TPU v7x, 256 devices: a whole 4x4x8 slice. The times are simulated.
256 devices in a mesh: attn: 16 (over z, core), ffn: 8 (over x, y_hi), grp: 2 (over y_lo).
Axes of the slice: x: 4, y: 4 (y_hi: 2, y_lo: 2; y = y_hi * 2 + y_lo), z: 8, core: 2. Of those that a mesh axis runs over, the one named last changes fastest.
Arguments:
- resid: bfloat16 [256, 12288], P('attn', ('ffn', 'grp')), may hold values from -6 to 6
- query: bfloat16 [256, 12288], P('attn', ('ffn', 'grp')), may hold values from -2.5 to 2.5
- key_new: bfloat16 [256, 12288], P('attn', ('ffn', 'grp')), may hold values from -2.5 to 2.5
- value_new: bfloat16 [256, 12288], P('attn', ('ffn', 'grp')), may hold values from -6 to 6
- key_cache: bfloat16 [256, 128, 12288], P('attn', None, ('ffn', 'grp')), may hold values from -2.5 to 2.5
- value_cache: bfloat16 [256, 128, 12288], P('attn', None, ('ffn', 'grp')), may hold values from -6 to 6
- lengths: int32 [256], P('attn'), may hold values from 1 to 128, as said below
- norm_gain: float32 [12288], replicated, may hold values from 0.5 to 1.5
- active: int32 [64, 64], replicated, may hold values from 0 to 255, all different within a row; in each aligned block of 4 rows (0 to 3, 4 to 7, ...) at most 2 rows name the same one
- up_weight: bfloat16 [12288, 32768], P(None, ('attn', 'ffn', 'grp')), may hold values from -0.0546875 to 0.0546875
- down_weight: bfloat16 [32768, 12288], P(('attn', 'ffn', 'grp')), may hold values from -0.0625 to 0.0625
Outputs:
- layer_out: bfloat16 [256, 12288], P('attn', ('ffn', 'grp'))
Inputs may be any that keep to these rules, and one draw needn't show every extreme that they name: `lengths`: some request has exactly 128 entries. `active`: each row names 64 different blocks; among the 4 row blocks of one attention index (rows a * 4 to a * 4 + 3) at most 2 name the same block, and some block is named by exactly 2 of them.
All inputs are finite; a program needn't handle non-finite values.
Results may differ from a plain program's by a relative error of at most 0.015.
Values may be sent and summed in bfloat16 or wider, within the bound.
A program may use at most 128 MiB of HBM per device.

v0:
```python
import jax
import jax.numpy as jnp
from jax import lax
from jax.sharding import PartitionSpec as P

HD = 128


def attend_rows(resid, query, key_new, value_new, key_cache, value_cache, lengths):
    requests, columns = resid.shape
    maxlen = key_cache.shape[1]
    heads_here = columns // HD
    scale = HD ** (-0.5)
    query_heads = query.reshape(requests, heads_here, HD)
    key_heads = key_cache.reshape(requests, maxlen, heads_here, HD)
    value_heads = value_cache.reshape(requests, maxlen, heads_here, HD)
    scores = (
        jnp.einsum("rhd,rjhd->rhj", query_heads, key_heads, preferred_element_type=jnp.float32)
        * scale
    )
    own_score = (
        jnp.einsum(
            "rhd,rhd->rh",
            query_heads,
            key_new.reshape(requests, heads_here, HD),
            preferred_element_type=jnp.float32,
        )
        * scale
    )
    positions = jnp.arange(maxlen, dtype=jnp.int32)
    usable = positions[None, None, :] < lengths[:, None, None]
    expo = jnp.where(usable, jnp.exp(scores), jnp.float32(0.0))
    own_exp = jnp.exp(own_score)
    denom = jnp.sum(expo, axis=-1) + own_exp
    weights = (expo / denom[:, :, None]).astype(jnp.bfloat16)
    own_weight = (own_exp / denom).astype(jnp.bfloat16)
    mixed = jnp.einsum("rhj,rjhd->rhd", weights, value_heads, preferred_element_type=jnp.float32)
    mixed = mixed + own_weight.astype(jnp.float32)[:, :, None] * value_new.reshape(
        requests, heads_here, HD
    ).astype(jnp.float32)
    return (resid.astype(jnp.float32) + mixed.reshape(requests, columns)).astype(jnp.bfloat16)


def feed_forward(stream, batch_index, local_total, norm_gain, active, up_weight, down_weight):
    half_rows = stream.shape[0]
    full_rows = lax.all_gather(stream, ("ffn", "grp"), axis=1, tiled=True)
    values = full_rows.astype(jnp.float32)
    mean_row = jnp.mean(values, axis=1, keepdims=True)
    centred = values - mean_row
    var_row = jnp.mean(centred * centred, axis=1, keepdims=True)
    normed = (centred * lax.rsqrt(var_row + 1e-05) * norm_gain[None, :]).astype(jnp.bfloat16)
    group_count = lax.axis_size(("ffn", "grp"))
    group_index = lax.axis_index(("ffn", "grp"))
    attn_count = lax.axis_size("attn")
    attn_index = lax.axis_index("attn")
    my_block = attn_index * group_count + group_index
    span_total = active.shape[0]
    spans_here = span_total // attn_count
    span_rows = local_total // spans_here
    span_hits = jnp.any(active == my_block, axis=1).astype(jnp.float32)
    piece_rows = lax.all_gather(normed, "attn", axis=0, tiled=True)
    row_ids = jnp.arange(piece_rows.shape[0], dtype=jnp.int32)
    source = row_ids // half_rows
    global_rows = source * local_total + batch_index * half_rows + row_ids % half_rows
    owner_table = (
        (global_rows // span_rows)[:, None] == jnp.arange(span_total, dtype=jnp.int32)[None, :]
    ).astype(jnp.float32)
    row_flags = jnp.dot(owner_table, span_hits, precision=lax.Precision.HIGHEST)
    before = jnp.dot(piece_rows, up_weight, preferred_element_type=jnp.float32)
    hidden_all = (jnp.maximum(before, 0.0) * row_flags[:, None]).astype(jnp.bfloat16)
    block_part = lax.psum_scatter(
        jnp.dot(hidden_all, down_weight, preferred_element_type=jnp.float32).astype(jnp.bfloat16),
        "attn",
        scatter_dimension=0,
        tiled=True,
    )
    summed = lax.psum_scatter(block_part, ("ffn", "grp"), scatter_dimension=1, tiled=True).astype(
        jnp.float32
    )
    return (stream.astype(jnp.float32) + summed).astype(jnp.bfloat16)


def shards(
    resid,
    query,
    key_new,
    value_new,
    key_cache,
    value_cache,
    lengths,
    norm_gain,
    active,
    up_weight,
    down_weight,
):
    local_total = resid.shape[0]
    half_rows = local_total // 2
    results = []
    for batch_index in range(2):
        first = batch_index * half_rows
        last = first + half_rows
        stream = attend_rows(
            resid[first:last],
            query[first:last],
            key_new[first:last],
            value_new[first:last],
            key_cache[first:last],
            value_cache[first:last],
            lengths[first:last],
        )
        results.append(
            feed_forward(
                stream, batch_index, local_total, norm_gain, active, up_weight, down_weight
            )
        )
    return jnp.concatenate(results, axis=0)


def solution(mesh):
    placed = (
        P("attn", ("ffn", "grp")),
        P("attn", ("ffn", "grp")),
        P("attn", ("ffn", "grp")),
        P("attn", ("ffn", "grp")),
        P("attn", None, ("ffn", "grp")),
        P("attn", None, ("ffn", "grp")),
        P("attn"),
        P(),
        P(),
        P(None, ("attn", "ffn", "grp")),
        P(("attn", "ffn", "grp"), None),
    )
    return jax.shard_map(
        shards, mesh=mesh, in_specs=placed, out_specs=P("attn", ("ffn", "grp")), check_vma=False
    )
```

profile of v0, /device:TPU:2, one launch (start us, length us, event | category | flops | bytes accessed | tf_op | source)
XLA Modules:
  0.0 455.8 jit_solution(12602714365285411308)
XLA Ops:
  6.5 0.9 fusion.57
  7.6 0.7 slice_bitcast_fusion.1
  8.3 0.8 fusion.31
  9.2 3.8 fusion.55
  13.0 2.6 copy.40
  15.6 2.6 copy.42
  18.1 2.1 fusion.40
  20.3 1.9 fusion.36
  22.5 1.9 fusion.56
  24.4 2.6 copy.41
  27.0 2.6 copy.43
  29.6 2.3 fusion.38
  31.9 2.3 fusion.34
  34.4 23.8 %all_gather.12 = bf16[8,12288]{1,0:T(8,128)(2,1)S(1)} all-gather(bf16[8,768]{1,0:T(8,128)(2,1)S(1)} %get-tuple-element.13), channel_id=1, replica_groups=mesh['attn'=16,'ffn'=8,'grp'=2] {'ffn','grp'}, dimensions={1}, use_global_device_ids=true | all-gather | bytes 208896 | tf_op jit(solution)/shard_map/all_gather | solution.py:46
  58.1 0.2 convert_reduce_fusion.1
  58.4 0.3 fusion.11
  58.7 21.9 %all_gather.14 = bf16[8,12288]{1,0:T(8,128)(2,1)S(1)} all-gather(bf16[8,768]{1,0:T(8,128)(2,1)S(1)} %get-tuple-element.14), channel_id=1, replica_groups=mesh['attn'=16,'ffn'=8,'grp'=2] {'ffn','grp'}, dimensions={1}, use_global_device_ids=true | all-gather | bytes 208896 | tf_op jit(solution)/shard_map/all_gather | solution.py:46
  80.6 0.2 convert_reduce_fusion
  80.8 0.3 fusion.8
  81.1 0.9 fusion.13
  82.1 0.7 all-gather.5.cloned.1.call-update
  83.2 41.6 %all-gather.3.cloned.1.call-done = bf16[128,12288]{1,0:T(8,128)(2,1)} async-done(((bf16[8,12288]{1,0:T(8,128)(2,1)}), bf16[128,12288]{1,0:T(8,128)(2,1)}) %all-gather.3.cloned.1.call-update) | async-done | bytes 3145744 | tf_op jit(solution)/shard_map/all_gather | solution.py:61
  124.8 6.4 %convolution_convert_fusion.1 = bf16[128,12288]{1,0:T(8,128)(2,1)} fusion(bf16[128,12288]{1,0:T(8,128)(2,1)S(1)} %copy-done, bf16[128,12288]{1,0:T(8,128)(2,1)} %all-gather.3.cloned.1.call-done, bf16[12288,128]{1,0:T(8,128)(2,1)} %param.20, f32[128]{0:T(128)S(1)} %convolution_bitcast_fusion.1), kind=kOutput, calls=%fused_computation.1 | convolution fusion | flops 806928384 | bytes 12583424 | tf_op jit(solution)/shard_map/dot_general | solution.py:72
  131.5 34.7 %all-gather.5.cloned.1.call-done = bf16[128,12288]{1,0:T(8,128)(2,1)} async-done(((bf16[8,12288]{1,0:T(8,128)(2,1)}), bf16[128,12288]{1,0:T(8,128)(2,1)}) %all-gather.5.cloned.1.call-update) | async-done | bytes 3145744 | tf_op jit(solution)/shard_map/all_gather | solution.py:61
  166.3 6.4 %convolution_convert_fusion = bf16[128,12288]{1,0:T(8,128)(2,1)} fusion(bf16[128,12288]{1,0:T(8,128)(2,1)S(1)} %copy-done, bf16[128,12288]{1,0:T(8,128)(2,1)} %all-gather.5.cloned.1.call-done, bf16[12288,128]{1,0:T(8,128)(2,1)} %param.20, f32[128]{0:T(128)S(1)} %convolution_bitcast_fusion), kind=kOutput, calls=%fused_computation | convolution fusion | flops 806928384 | bytes 12583424 | tf_op jit(solution)/shard_map/dot_general | solution.py:72
  172.8 55.7 %reduce-scatter.5.cloned.1.call-done = bf16[8,12288]{1,0:T(8,128)(2,1)} async-done(((bf16[128,12288]{1,0:T(8,128)(2,1)}), bf16[8,12288]{1,0:T(8,128)(2,1)}) %reduce-scatter.5.cloned.1.call-update) | async-done | bytes 196624 | tf_op jit(solution)/shard_map/reduce_scatter | solution.py:71
  228.6 61.8 %reduce-scatter.9.cloned.1.call-done = bf16[8,12288]{1,0:T(8,128)(2,1)} async-done(((bf16[128,12288]{1,0:T(8,128)(2,1)}), bf16[8,12288]{1,0:T(8,128)(2,1)}) %reduce-scatter.9.cloned.1.call-update) | async-done | bytes 196624 | tf_op jit(solution)/shard_map/reduce_scatter | solution.py:71
  290.4 77.8 %reduce-scatter.7.cloned.1.call-done = bf16[8,768]{1,0:T(8,128)(2,1)} async-done(((bf16[8,12288]{1,0:T(8,128)(2,1)}), bf16[8,768]{1,0:T(8,128)(2,1)}) %reduce-scatter.7.cloned.1.call-update) | async-done | bytes 12304 | tf_op jit(solution)/shard_map/reduce_scatter | solution.py:77
  368.2 0.7 add_convert_fusion.1
  368.9 78.7 %reduce-scatter.11.cloned.1.call-done = bf16[8,768]{1,0:T(8,128)(2,1)} async-done(((bf16[8,12288]{1,0:T(8,128)(2,1)}), bf16[8,768]{1,0:T(8,128)(2,1)}) %reduce-scatter.11.cloned.1.call-update) | async-done | bytes 12304 | tf_op jit(solution)/shard_map/reduce_scatter | solution.py:77
  447.6 0.7 add_convert_fusion
  448.4 0.6 pad_maximum_fusion
  (40 shorter events, 1.5 us)
Async XLA Ops:
  6.5 118.3 %copy-start = (bf16[128,12288]{1,0:T(8,128)(2,1)S(1)}, bf16[128,12288]{1,0:T(8,128)(2,1)}, u32[]{:S(2)}) copy-start(bf16[128,12288]{1,0:T(8,128)(2,1)} %param.21) | copy-start | bytes 9437188
  6.5 118.3 %all-gather.3.cloned.1.call-start = ((), (), s32[]{:S(2)}) async-start(), calls=%async_computation.4 | async-start | bytes 3342336 | tf_op jit(solution)/shard_map/all_gather | solution.py:61
  18.1 4.4 copy-start.1
  27.0 7.2 %copy-start.4 = (bf16[16,768]{1,0:T(8,128)(2,1)S(1)}, bf16[16,768]{1,0:T(8,128)(2,1)}, u32[]{:S(2)}) copy-start(bf16[16,768]{1,0:T(8,128)(2,1)} %param.14) | copy-start | bytes 73732
  27.0 7.2 %copy-start.5 = (bf16[16,768]{1,0:T(8,128)(2,1)S(1)}, bf16[16,768]{1,0:T(8,128)(2,1)}, u32[]{:S(2)}) copy-start(bf16[16,768]{1,0:T(8,128)(2,1)} %param.11) | copy-start | bytes 73732
  27.0 54.1 %copy-start.2 = (f32[12288]{0:T(1024)S(1)}, f32[12288]{0:T(1024)}, u32[]{:S(2)}) copy-start(f32[12288]{0:T(1024)} %param.18) | copy-start | bytes 147460
  29.6 53.3 %copy-start.3 = (s32[64,64]{1,0:T(8,128)S(1)}, s32[64,64]{1,0:T(8,128)}, u32[]{:S(2)}) copy-start(s32[64,64]{1,0:T(8,128)} %param.19) | copy-start | bytes 49156
  82.0 84.3 %all-gather.5.cloned.1.call-start = ((), (), s32[]{:S(2)}) async-start(), calls=%async_computation.7 | async-start | bytes 3342336 | tf_op jit(solution)/shard_map/all_gather | solution.py:61
  82.8 145.7 %reduce-scatter.5.cloned.1.call-start = ((), (), s32[]{:S(2)}) async-start(), calls=%async_computation.5 | async-start | bytes 3342336 | tf_op jit(solution)/shard_map/reduce_scatter | solution.py:71
  131.3 159.1 %reduce-scatter.9.cloned.1.call-start = ((), (), s32[]{:S(2)}) async-start(), calls=%async_computation.8 | async-start | bytes 3342336 | tf_op jit(solution)/shard_map/reduce_scatter | solution.py:71
  172.8 195.5 %reduce-scatter.7.cloned.1.call-start = ((), (), s32[]{:S(2)}) async-start(), calls=%async_computation.6 | async-start | bytes 208896 | tf_op jit(solution)/shard_map/reduce_scatter | solution.py:77
  228.5 219.1 %reduce-scatter.11.cloned.1.call-start = ((), (), s32[]{:S(2)}) async-start(), calls=%async_computation.9 | async-start | bytes 208896 | tf_op jit(solution)/shard_map/reduce_scatter | solution.py:77
Sparse Core Ops, SparseCore 0:
  82.2 42.6 all-gather.2
  126.6 39.5 all-gather.4
  168.8 59.5 reduce-scatter.4
  230.9 59.4 reduce-scatter.8
  293.7 74.4 reduce-scatter.6
  372.0 75.6 reduce-scatter.10
where the time goes:
time: 456 us
  waiting for transfers between devices  351 us (77%)
  blocking collectives  45.7 us (10%)
  matrix products  21.9 us (5%)
  local copies, waits for them, and re-layouts  17.7 us (4%)
  between operations  13.6 us (3%)
  other arithmetic  5.6 us (1%)
    reduce_scatter x2, waiting for transfers between devices, feed_forward(): lax.psum_scatter(block_part, ('ffn', 'grp'), scatter_dimension=1, tiled=T...  156 us
    reduce_scatter x2, waiting for transfers between devices, feed_forward(): lax.psum_scatter(jnp.dot(hidden_all, down_weight, preferred_element_type=...  118 us
    all_gather x2, waiting for transfers between devices, feed_forward(): piece_rows = lax.all_gather(normed, 'attn', axis=0, tiled=True)  76.4 us
    all_gather x2, blocking collectives, feed_forward(): full_rows = lax.all_gather(stream, ('ffn', 'grp'), axis=1, tiled=True)  45.7 us
    dot_general x2, matrix products, feed_forward(): jnp.dot(hidden_all, down_weight, preferred_element_type=jnp.float32)  12.9 us
    unnamed x16, local copies, waits for them, and re-layouts  10.4 us
  transfers between devices with their start and end apart: 6, of which 6 were waited for; matrix products, arithmetic and copies ran while one was open for 3% of the time, Pallas kernels for 0%

commit v1 on v0

v1 whole, which is shorter than its diff:
```python
import functools

import jax
import jax.numpy as jnp
from jax import lax
from jax.experimental import pallas as pl
from jax.experimental.pallas import tpu as pltpu
from jax.sharding import PartitionSpec as P

MESH = pl.DeviceIdType.MESH
HD = 128
BF = jnp.bfloat16
F32 = jnp.float32
NT = (((1,), (1,)), ((), ()))
R = 16
NZ = 8
ROWS = R * NZ
HALF = ROWS // 2
STEP = 4


def attend_kernel(len_ref, resid_ref, q_ref, kn_ref, vn_ref, k_ref, v_ref, out_ref, qf, knf, vnf, att):
    at = pl.program_id(0)
    cols = resid_ref.shape[1]
    scale = HD ** (-0.5)

    @pl.when(at == 0)
    def _():
        qf[...] = q_ref[...].astype(F32)
        knf[...] = kn_ref[...].astype(F32)
        vnf[...] = vn_ref[...].astype(F32)

    head_of = lax.broadcasted_iota(jnp.int32, (8, cols), 1) // HD
    mine = head_of == lax.broadcasted_iota(jnp.int32, (8, cols), 0)
    place = lax.broadcasted_iota(jnp.int32, (8, HD), 1)
    for t in range(STEP):
        r = at * STEP + t
        heads = jnp.where(mine, qf[pl.ds(r, 1), :], 0.0)
        scores = lax.dot_general(heads.astype(BF), k_ref[t], NT, preferred_element_type=F32) * scale
        own = jnp.sum(heads * knf[pl.ds(r, 1), :], axis=1, keepdims=True) * scale
        expo = jnp.where(place < len_ref[r], jnp.exp(scores), 0.0)
        own_exp = jnp.exp(own)
        denom = jnp.sum(expo, axis=1, keepdims=True) + own_exp
        weights = (expo / denom).astype(BF)
        own_weight = (own_exp / denom).astype(BF).astype(F32)
        mixed = jnp.dot(weights, v_ref[t], preferred_element_type=F32) + own_weight * vnf[pl.ds(r, 1), :]
        att[pl.ds(r, 1), :] = jnp.sum(jnp.where(mine, mixed, 0.0), axis=0, keepdims=True)

    @pl.when(at == pl.num_programs(0) - 1)
    def _():
        out_ref[...] = (resid_ref[...].astype(F32) + att[...]).astype(BF)


def attend(resid, query, key_new, value_new, key_cache, value_cache, lengths):
    cols = resid.shape[1]
    whole = pl.BlockSpec((R, cols), lambda i: (0, 0))
    cache = pl.BlockSpec((STEP, 128, cols), lambda i: (i, 0, 0))
    return pl.pallas_call(
        attend_kernel,
        grid=(R // STEP,),
        out_shape=jax.ShapeDtypeStruct((R, cols), BF),
        in_specs=[pl.BlockSpec(memory_space=pltpu.SMEM), whole, whole, whole, whole, cache, cache],
        out_specs=whole,
        scratch_shapes=[pltpu.VMEM((R, cols), F32)] * 4,
        compiler_params=pltpu.CompilerParams(vmem_limit_bytes=32 * 1024 * 1024),
        name="attend",
    )(lengths, resid, query, key_new, value_new, key_cache, value_cache)


def ffn_kernel(
    stream_ref, gain_ref, active_ref, up_ref, down_ref, out_ref,
    xbuf, wu, wd, stats, rowsf,
    ya, yr, yl, ra, rl, rr, pa, pr, pleft, qa, ql, qr, tz, rz,
    w_loc, w_send, w_recv, st_send, st_recv, z_send, z_recv, p1_send, p1_recv, p2_send, p2_recv,
    a_send, a_recv, b_send, b_recv, c_send, c_recv, zz_send, zz_recv,
):
    attn, ffn, grp = lax.axis_index("attn"), lax.axis_index("ffn"), lax.axis_index("grp")
    z, core = attn // 2, attn % 2
    x, y = ffn // 2, (ffn % 2) * 2 + grp
    other = 1 - core
    p1 = x * other + y * core
    p2 = y * other + x * core
    cols = stream_ref.shape[1]
    width = 16 * cols

    def place(z_at, core_at, x_at, y_at):
        return (z_at * 2 + core_at, x_at * 2 + y_at // 2, y_at % 2)

    def near(i, j):
        q2, q1 = (p2 + i) % 4, (p1 + j) % 4
        return place(z, core, q1 * other + q2 * core, q2 * other + q1 * core)

    def group(i, j):
        q2, q1 = (p2 + i) % 4, (p1 + j) % 4
        return (q1 * other + q2 * core) * 4 + q2 * other + q1 * core

    def slot(i, j):
        return xbuf.at[(p2 + i) % 4, (p1 + j) % 4]

    def send(src, dst, s_sem, r_sem, device):
        copy = pltpu.make_async_remote_copy(
            src_ref=src, dst_ref=dst, send_sem=s_sem, recv_sem=r_sem, device_id=device, device_id_type=MESH
        )
        copy.start()
        started.append(copy)
        return copy

    def arrived(dst, r_sem):
        pltpu.make_async_remote_copy(
            src_ref=dst, dst_ref=dst, send_sem=r_sem, recv_sem=r_sem, device_id=near(0, 1), device_id_type=MESH
        ).wait_recv()

    started = []
    up_here = pltpu.make_async_copy(up_ref, wu.at[core], w_loc.at[0])
    up_here.start()
    down_rows = pl.ds(pl.multiple_of(core * 128, 128), 128)
    down_other = pl.ds(pl.multiple_of(other * 128, 128), 128)
    down_here = pltpu.make_async_copy(down_ref, wd.at[down_rows], w_loc.at[1])
    down_here.start()

    plane = [(i, j) for i in range(4) for j in range(4) if (i, j) != (0, 0)]
    barrier = pltpu.get_barrier_semaphore()
    partner = place(z, other, x, y)
    for i, j in plane:
        pl.semaphore_signal(barrier, inc=1, device_id=near(i, j), device_id_type=MESH)
    for k in range(1, NZ):
        pl.semaphore_signal(barrier, inc=1, device_id=place((z + k) % NZ, core, x, y), device_id_type=MESH)
    pl.semaphore_signal(barrier, inc=1, device_id=partner, device_id_type=MESH)
    pl.semaphore_wait(barrier, len(plane) + NZ)

    values = stream_ref[...].astype(F32)
    eye = (
        lax.broadcasted_iota(jnp.int32, (R, 128), 0) == lax.broadcasted_iota(jnp.int32, (R, 128), 1)
    ).astype(F32)
    own_mean = jnp.mean(values, axis=1, keepdims=True)
    off = values - own_mean
    own_sq = jnp.sum(off * off, axis=1, keepdims=True)
    here = stats.at[group(0, 0)]
    here[0:1, :] = jnp.sum(own_mean * eye, axis=0, keepdims=True)
    here[1:2, :] = jnp.sum(own_sq * eye, axis=0, keepdims=True)
    for n, (i, j) in enumerate(plane):
        send(here, here, st_send.at[n], st_recv.at[n], near(i, j))
    up_there = send(up_ref, wu.at[core], w_send.at[0], w_recv.at[0], partner)
    down_there = send(down_ref, wd.at[down_rows], w_send.at[1], w_recv.at[1], partner)
    for n, (i, j) in enumerate(plane):
        arrived(stats.at[group(4 - i, 4 - j)], st_recv.at[n])
    means, squares = stats[:, 0, :], stats[:, 1, :]
    mean_all = jnp.sum(means, axis=0, keepdims=True) * (1.0 / 16)
    gap = means - mean_all
    var_all = (jnp.sum(squares, axis=0, keepdims=True) + cols * jnp.sum(gap * gap, axis=0, keepdims=True)) * (
        1.0 / width
    )
    mean_row = jnp.sum(mean_all * eye, axis=1, keepdims=True)
    rstd_row = jnp.sum(lax.rsqrt(var_all + 1e-05) * eye, axis=1, keepdims=True)
    gain = gain_ref[pl.ds(group(0, 0), 1), :]
    z_rows = pl.ds(pl.multiple_of(z * R, R), R)
    mine = slot(0, 0)
    mine[z_rows, :] = ((values - mean_row) * rstd_row * gain).astype(BF)

    for k in range(1, NZ):
        send(mine.at[z_rows], mine.at[z_rows], z_send.at[k - 1], z_recv.at[k - 1], place((z + k) % NZ, core, x, y))

    block0 = z * 32 + group(0, 0)
    hit0 = jnp.max((active_ref[...] == block0).astype(F32), axis=1, keepdims=True)
    hit1 = jnp.max((active_ref[...] == block0 + 16).astype(F32), axis=1, keepdims=True)
    spans = active_ref.shape[0]
    hits = jnp.concatenate([jnp.broadcast_to(hit0, (spans, 128)), jnp.broadcast_to(hit1, (spans, 128))], axis=1)
    row_at = lax.broadcasted_iota(jnp.int32, (ROWS, spans), 0)
    span_at = lax.broadcasted_iota(jnp.int32, (ROWS, spans), 1)
    span_of = ((row_at // R) * 2 + core) * 4 + (row_at % R) // 4
    row_mask = jnp.dot((span_of == span_at).astype(BF), hits.astype(BF), preferred_element_type=F32)

    for k in range(1, NZ):
        from_rows = pl.ds(pl.multiple_of(((z + NZ - k) % NZ) * R, R), R)
        arrived(mine.at[from_rows], z_recv.at[k - 1])

    first, second = pl.ds(0, HALF), pl.ds(HALF, HALF)

    def spread(j):
        send(slot(0, j), slot(0, j), p2_send.at[0, j], p2_recv.at[0, j], near(1, 0))
        send(slot(0, j), slot(0, j), p2_send.at[1, j], p2_recv.at[1, j], near(3, 0))

    send(mine, mine, p1_send.at[0], p1_recv.at[0], near(0, 1))
    send(mine, mine, p1_send.at[1], p1_recv.at[1], near(0, 3))
    spread(0)
    up_here.wait()
    arrived(wu.at[other], w_recv.at[0])

    def up(i, j):
        rows = pl.ds(pl.multiple_of(group(i, j) * cols, 128), cols)
        both = jnp.concatenate([wu[0, rows, :], wu[1, rows, :]], axis=1)
        return jnp.dot(slot(i, j)[...], both, preferred_element_type=F32)

    before = up(0, 0)
    arrived(slot(0, 3), p1_recv.at[0])
    send(slot(0, 3).at[first], slot(0, 3).at[first], p1_send.at[2], p1_recv.at[2], near(0, 1))
    spread(3)
    arrived(slot(0, 1), p1_recv.at[1])
    send(slot(0, 1).at[second], slot(0, 1).at[second], p1_send.at[3], p1_recv.at[3], near(0, 3))
    spread(1)
    before += up(0, 3)
    before += up(0, 1)
    arrived(slot(0, 2).at[first], p1_recv.at[2])
    arrived(slot(0, 2).at[second], p1_recv.at[3])
    spread(2)
    before += up(0, 2)
    order = (0, 3, 1, 2)
    for j in order:
        arrived(slot(3, j), p2_recv.at[0, j])
        send(slot(3, j).at[first], slot(3, j).at[first], p2_send.at[2, j], p2_recv.at[2, j], near(1, 0))
        arrived(slot(1, j), p2_recv.at[1, j])
        send(slot(1, j).at[second], slot(1, j).at[second], p2_send.at[3, j], p2_recv.at[3, j], near(3, 0))
        before += up(3, j)
        before += up(1, j)
    for j in order:
        arrived(slot(2, j).at[first], p2_recv.at[2, j])
        arrived(slot(2, j).at[second], p2_recv.at[3, j])
        before += up(2, j)
    hidden = (jnp.maximum(before, 0.0) * row_mask).astype(BF)

    down_here.wait()
    arrived(wd.at[down_other], w_recv.at[1])

    def down(i, j):
        columns = pl.ds(pl.multiple_of(group(i, j) * cols, 128), cols)
        return jnp.dot(hidden, wd[:, columns], preferred_element_type=F32)

    back = (2, 3, 1, 0)
    for j in back:
        ya[j] = down(2, j).astype(BF)
        send(ya.at[j, first], ra.at[j, first], a_send.at[0, j], a_recv.at[0, j], near(1, 0))
        send(ya.at[j, second], ra.at[j, second], a_send.at[1, j], a_recv.at[1, j], near(3, 0))
    for j in back:
        part = down(1, j)
        yr[j, HALF:] = part[HALF:].astype(BF)
        arrived(ra.at[j, first], a_recv.at[0, j])
        yr[j, :HALF] = (part[:HALF] + ra[j, :HALF].astype(F32)).astype(BF)
        send(yr.at[j], rl.at[j], b_send.at[0, j], b_recv.at[0, j], near(1, 0))
        part = down(3, j)
        yl[j, :HALF] = part[:HALF].astype(BF)
        arrived(ra.at[j, second], a_recv.at[1, j])
        yl[j, HALF:] = (part[HALF:] + ra[j, HALF:].astype(F32)).astype(BF)
        send(yl.at[j], rr.at[j], b_send.at[1, j], b_recv.at[1, j], near(3, 0))

    def settled(j):
        part = down(0, j)
        arrived(rl.at[j], b_recv.at[0, j])
        part += rl[j].astype(F32)
        arrived(rr.at[j], b_recv.at[1, j])
        return part + rr[j].astype(F32)

    pa[...] = settled(2).astype(BF)
    send(pa.at[first], qa.at[first], c_send.at[0], c_recv.at[0], near(0, 1))
    send(pa.at[second], qa.at[second], c_send.at[1], c_recv.at[1], near(0, 3))
    part = settled(3)
    pleft[:HALF] = part[:HALF].astype(BF)
    arrived(qa.at[second], c_recv.at[1])
    pleft[HALF:] = (part[HALF:] + qa[HALF:].astype(F32)).astype(BF)
    send(pleft, qr, c_send.at[3], c_recv.at[3], near(0, 3))
    part = settled(1)
    pr[HALF:] = part[HALF:].astype(BF)
    arrived(qa.at[first], c_recv.at[0])
    pr[:HALF] = (part[:HALF] + qa[:HALF].astype(F32)).astype(BF)
    send(pr, ql, c_send.at[2], c_recv.at[2], near(0, 1))
    part = settled(0)
    arrived(ql, c_recv.at[2])
    part += ql[...].astype(F32)
    arrived(qr, c_recv.at[3])
    part += qr[...].astype(F32)
    rowsf[...] = part
    tz[...] = part.astype(BF)
    for k in range(1, NZ):
        to_rows = pl.ds(pl.multiple_of(((z + k) % NZ) * R, R), R)
        send(tz.at[to_rows], rz.at[k - 1], zz_send.at[k - 1], zz_recv.at[k - 1], place((z + k) % NZ, core, x, y))
    total = rowsf[z_rows, :]
    for k in range(1, NZ):
        arrived(rz.at[k - 1], zz_recv.at[k - 1])
        total += rz[k - 1].astype(F32)
    out_ref[...] = (values + total).astype(BF)
    for copy in started:
        copy.wait_send()


def feed_forward(stream, norm_gain, active, up_weight, down_weight):
    cols = stream.shape[1]
    width = 16 * cols
    vmem = pl.BlockSpec(memory_space=pltpu.VMEM)
    hbm = pl.BlockSpec(memory_space=pl.ANY)
    dma = pltpu.SemaphoreType.DMA
    full = pltpu.VMEM((ROWS, cols), BF)
    four = pltpu.VMEM((4, ROWS, cols), BF)
    return pl.pallas_call(
        ffn_kernel,
        out_shape=jax.ShapeDtypeStruct((R, cols), BF),
        in_specs=[vmem, vmem, vmem, hbm, hbm],
        out_specs=vmem,
        scratch_shapes=[
            pltpu.VMEM((4, 4, ROWS, cols), BF),
            pltpu.VMEM((2, width, 128), BF),
            pltpu.VMEM((256, width), BF),
            pltpu.VMEM((16, 2, 128), F32),
            pltpu.VMEM((ROWS, cols), F32),
            four, four, four, four, four, four,
            full, full, full, full, full, full, full,
            pltpu.VMEM((NZ - 1, R, cols), BF),
            dma((2,)), dma((2,)), dma((2,)),
            dma((15,)), dma((15,)),
            dma((NZ - 1,)), dma((NZ - 1,)),
            dma((4,)), dma((4,)),
            dma((4, 4)), dma((4, 4)),
            dma((2, 4)), dma((2, 4)), dma((2, 4)), dma((2, 4)),
            dma((4,)), dma((4,)),
            dma((NZ - 1,)), dma((NZ - 1,)),
        ],
        compiler_params=pltpu.CompilerParams(
            collective_id=0, has_side_effects=True, vmem_limit_bytes=56 * 1024 * 1024
        ),
        name="gather_ffn_scatter",
    )(stream, norm_gain.reshape(16, cols), active, up_weight, down_weight)


def shards(
    resid, query, key_new, value_new, key_cache, value_cache, lengths, norm_gain, active, up_weight, down_weight
):
    stream = attend(resid, query, key_new, value_new, key_cache, value_cache, lengths)
    return feed_forward(stream, norm_gain, active, up_weight, down_weight)


def solution(mesh):
    placed = (
        P("attn", ("ffn", "grp")),
        P("attn", ("ffn", "grp")),
        P("attn", ("ffn", "grp")),
        P("attn", ("ffn", "grp")),
        P("attn", None, ("ffn", "grp")),
        P("attn", None, ("ffn", "grp")),
        P("attn"),
        P(),
        P(),
        P(None, ("attn", "ffn", "grp")),
        P(("attn", "ffn", "grp"), None),
    )
    return jax.shard_map(
        shards, mesh=mesh, in_specs=placed, out_specs=P("attn", ("ffn", "grp")), check_vma=False
    )
```

time: 456 us -> 90.4 us (0.20)
  waiting for transfers between devices: 351 us -> 0 us
  Pallas kernels: 0 us -> 79.7 us
  blocking collectives: 45.7 us -> 0 us
  matrix products: 21.9 us -> 0 us
  between operations: 13.6 us -> 0.03 us
  local copies, waits for them, and re-layouts: 17.7 us -> 9.96 us
  other arithmetic: 5.6 us -> 0 us
    reduce_scatter x4 -> x0, waiting for transfers between devices: 274 us -> none  [the longest x2 156 us: feed_forward(): lax.psum_scatter(block_part, ('ffn', 'grp'), scatter_dimension=1, tiled=T...]
    pallas_call x0 -> x2, Pallas kernels: none -> 79.7 us  [the longest x1 73 us: feed_forward(): pl.pallas_call(ffn_kernel, out_shape=jax.ShapeDtypeStruct((R, cols), BF),...]
    all_gather x2 -> x0, waiting for transfers between devices: 76.4 us -> none  [feed_forward(): piece_rows = lax.all_gather(normed, 'attn', axis=0, tiled=True)]
    all_gather x2 -> x0, blocking collectives: 45.7 us -> none  [feed_forward(): full_rows = lax.all_gather(stream, ('ffn', 'grp'), axis=1, tiled=True)]
    dot_general x8 -> x0, matrix products: 21.9 us -> none  [the longest x2 12.9 us: feed_forward(): jnp.dot(hidden_all, down_weight, preferred_element_type=jnp.float32)]
    slice x3 -> x0, local copies, waits for them, and re-layouts: 6.58 us -> none  [the longest x1 3.82 us: shards(): key_cache[first:last]]
    unnamed x16 -> x19, local copies, waits for them, and re-layouts: 10.4 us -> 9.33 us
  transfers between devices with their start and end apart: 6 -> 0, of which waited for: 6 -> 0; matrix products, arithmetic and copies ran while one was open for 3% -> 0% of each run, Pallas kernels for 0% -> 0%
where the time goes in v1:
time: 90.4 us; the launch traced here: 89.6 us
  Pallas kernels  79.7 us (88%)
  local copies, waits for them, and re-layouts  9.96 us (11%)
    pallas_call x1, Pallas kernels, feed_forward(): pl.pallas_call(ffn_kernel, out_shape=jax.ShapeDtypeStruct((R, cols), BF),...  73 us
    unnamed x19, local copies, waits for them, and re-layouts  9.33 us
    pallas_call x1, Pallas kernels, attend(): pl.pallas_call(attend_kernel, grid=(R // STEP,), out_shape=jax.ShapeDtype...  6.62 us

profile of v1, /device:TPU:2, one launch (start us, length us, event | category | flops | bytes accessed | tf_op | source)
XLA Modules:
  0.0 89.6 jit_solution(7405904242510253918)
XLA Ops:
  0.0 0.0 copy-start
  0.0 1.9 %copy-done = bf16[16,128,768]{2,1,0:T(8,128)(2,1)S(1)} copy-done((bf16[16,128,768]{2,1,0:T(8,128)(2,1)S(1)}, bf16[16,128,768]{2,1,0:T(8,128)(2,1)}, u32[]{:S(2)}) %copy-start) | copy-done | bytes 3145752
  1.9 0.0 copy-start.1
  1.9 1.9 %copy-done.1 = bf16[16,128,768]{2,1,0:T(8,128)(2,1)S(1)} copy-done((bf16[16,128,768]{2,1,0:T(8,128)(2,1)S(1)}, bf16[16,128,768]{2,1,0:T(8,128)(2,1)}, u32[]{:S(2)}) %copy-start.1) | copy-done | bytes 3145752
  3.8 0.0 copy-start.3
  3.8 0.7 copy-done.3
  4.5 0.0 copy-start.4
  4.5 0.7 copy-done.4
  5.3 0.0 copy-start.5
  5.3 0.7 copy-done.5
  6.0 0.0 copy-start.6
  6.0 0.7 copy-done.6
  6.7 0.0 copy-start.7
  6.7 0.7 copy-done.7
  7.4 0.0 copy-start.8
  7.4 6.6 %attend.1.stream_ref = bf16[16,768]{1,0:T(8,128)(2,1)S(1)} custom-call(s32[16]{0:T(128)S(1)} %copy-done.7, bf16[16,768]{1,0:T(8,128)(2,1)S(1)} %copy-done.3, bf16[16,768]{1,0:T(8,128)(2,1)S(1)} %copy-done.4, bf16[16,768]{1,0:T(8,128)(2,1)S(1)} %copy-done.5, bf16[16,768]{1,0:T(8,128)(2,1)S(1)} %copy-done.6, bf16[16,128,768]{2,1,0:T(8,128)(2,1)S(1)} %copy-done, ...), custom_call_target="tpu_custom_call" | custom-call | tf_op jit(solution)/shard_map/attend/pallas_call | solution.py:58
  14.0 0.0 copy-start.2
  14.0 0.6 copy-done.2
  14.6 0.0 copy-done.8
  14.6 0.6 reshape.3.gain_ref
  15.3 73.0 %gather_ffn_scatter.1 = bf16[16,768]{1,0:T(8,128)(2,1)} custom-call(bf16[16,768]{1,0:T(8,128)(2,1)} %copy-done.2, f32[16,768]{1,0:T(8,128)} %reshape.3.gain_ref, s32[64,64]{1,0:T(8,128)} %active_ref.1, bf16[12288,128]{1,0:T(8,128)(2,1)} %up_ref.1, bf16[128,12288]{1,0:T(8,128)(2,1)} %down_ref.1), custom_call_target="tpu_custom_call" | custom-call | tf_op jit(solution)/shard_map/gather_ffn_scatter/pallas_call | solution.py:292
  88.3 1.3 %copy.13 = bf16[16,768]{1,0:T(8,128)(2,1)} copy(bf16[16,768]{1,0:T(8,128)(2,1)} %gather_ffn_scatter.1) | data formatting | bytes 49152
Async XLA Ops:
  0.0 1.9 %copy-start = (bf16[16,128,768]{2,1,0:T(8,128)(2,1)S(1)}, bf16[16,128,768]{2,1,0:T(8,128)(2,1)}, u32[]{:S(2)}) copy-start(bf16[16,128,768]{2,1,0:T(8,128)(2,1)} %k_ref.1) | copy-start | bytes 9437188
  1.9 1.9 %copy-start.1 = (bf16[16,128,768]{2,1,0:T(8,128)(2,1)S(1)}, bf16[16,128,768]{2,1,0:T(8,128)(2,1)}, u32[]{:S(2)}) copy-start(bf16[16,128,768]{2,1,0:T(8,128)(2,1)} %v_ref.1) | copy-start | bytes 9437188
  3.8 0.7 copy-start.3
  4.5 0.7 copy-start.4
  5.3 0.7 copy-start.5
  6.0 0.7 copy-start.6
  6.7 0.7 copy-start.7
  7.4 7.2 %copy-start.8 = (f32[12288]{0:T(1024)S(1)}, f32[12288]{0:T(1024)}, u32[]{:S(2)}) copy-start(f32[12288]{0:T(1024)} %param.18) | copy-start | bytes 147460
  14.0 0.6 copy-start.2

commit v2 on v1

v2 whole, which is shorter than its diff:
```python
import jax
import jax.numpy as jnp
from jax import lax
from jax.experimental import pallas as pl
from jax.experimental.pallas import tpu as pltpu
from jax.sharding import PartitionSpec as P

MESH = pl.DeviceIdType.MESH
HD = 128
BF = jnp.bfloat16
F32 = jnp.float32
NT = (((1,), (1,)), ((), ()))
R = 16
NZ = 8
ROWS = R * NZ
HALF = ROWS // 2
QUART = HALF // 2
DIST = (0, 1, 7, 2, 6, 3, 5, 4)
STEP = 4


def layer_kernel(
    resid_ref, q_ref, kn_ref, vn_ref, k_ref, v_ref, len_ref, gain_ref, active_ref, up_ref, down_ref, out_ref,
    resid_s, q_s, kn_s, vn_s, k_s, v_s, len_s, gain_s, active_s, qf, knf, vnf, att,
    xbuf, wu, wd, stats,
    ya, yr, yl, ra, rl, rr, pa, pr, pleft, qa, ql, qr, tz, rz,
    in_sem, k_sem, v_sem, w_loc, w_send, w_recv, st_send, st_recv, z_send, z_recv, p1_send, p1_recv, p2_send, p2_recv,
    a_send, a_recv, b_send, b_recv, c_send, c_recv, zz_send, zz_recv,
):
    attn, ffn, grp = lax.axis_index("attn"), lax.axis_index("ffn"), lax.axis_index("grp")
    z, core = attn // 2, attn % 2
    x, y = ffn // 2, (ffn % 2) * 2 + grp
    other = 1 - core
    p1 = x * other + y * core
    p2 = y * other + x * core
    cols = resid_ref.shape[1]
    width = 16 * cols

    def place(z_at, core_at, x_at, y_at):
        return (z_at * 2 + core_at, x_at * 2 + y_at // 2, y_at % 2)

    def near(i, j):
        q2, q1 = (p2 + i) % 4, (p1 + j) % 4
        return place(z, core, q1 * other + q2 * core, q2 * other + q1 * core)

    def along_z(k):
        return place((z + k) % NZ, core, x, y)

    def group(i, j):
        q2, q1 = (p2 + i) % 4, (p1 + j) % 4
        return (q1 * other + q2 * core) * 4 + q2 * other + q1 * core

    def slot(i, j):
        return xbuf.at[(p2 + i) % 4, (p1 + j) % 4]

    started = []

    def send(src, dst, s_sem, r_sem, device):
        copy = pltpu.make_async_remote_copy(
            src_ref=src, dst_ref=dst, send_sem=s_sem, recv_sem=r_sem, device_id=device, device_id_type=MESH
        )
        copy.start()
        started.append(copy)

    def arrived(dst, r_sem):
        pltpu.make_async_remote_copy(
            src_ref=dst, dst_ref=dst, send_sem=r_sem, recv_sem=r_sem, device_id=near(0, 1), device_id_type=MESH
        ).wait_recv()

    def fetch(src, dst, sem):
        copy = pltpu.make_async_copy(src, dst, sem)
        copy.start()
        return copy

    small = [
        fetch(src, dst, in_sem.at[n])
        for n, (src, dst) in enumerate(
            [(q_ref, q_s), (kn_ref, kn_s), (len_ref, len_s), (vn_ref, vn_s), (resid_ref, resid_s),
             (gain_ref, gain_s), (active_ref, active_s)]
        )
    ]
    steps = [pl.ds(n * STEP, STEP) for n in range(R // STEP)]
    keys_in = [fetch(k_ref.at[rows], k_s.at[rows], k_sem.at[n]) for n, rows in enumerate(steps)]
    values_in = [fetch(v_ref.at[rows], v_s.at[rows], v_sem.at[n]) for n, rows in enumerate(steps)]

    plane = [(i, j) for i in range(4) for j in range(4) if (i, j) != (0, 0)]
    barrier = pltpu.get_barrier_semaphore()
    partner = place(z, other, x, y)
    for i, j in plane:
        pl.semaphore_signal(barrier, inc=1, device_id=near(i, j), device_id_type=MESH)
    for k in range(1, NZ):
        pl.semaphore_signal(barrier, inc=1, device_id=along_z(k), device_id_type=MESH)
    pl.semaphore_signal(barrier, inc=1, device_id=partner, device_id_type=MESH)

    scale = HD ** (-0.5)
    head_of = lax.broadcasted_iota(jnp.int32, (8, cols), 1) // HD
    mine_head = head_of == lax.broadcasted_iota(jnp.int32, (8, cols), 0)
    position = lax.broadcasted_iota(jnp.int32, (8, HD), 1)
    for copy in small[:3]:
        copy.wait()
    qf[...] = q_s[...].astype(F32)
    knf[...] = kn_s[...].astype(F32)
    weights, own_weights = [], []
    for n in range(R // STEP):
        requests = range(n * STEP, (n + 1) * STEP)
        heads = [jnp.where(mine_head, qf[r : r + 1, :], 0.0) for r in requests]
        own = [
            jnp.exp(jnp.sum(head * knf[r : r + 1, :], axis=1, keepdims=True) * scale)
            for r, head in zip(requests, heads)
        ]
        keys_in[n].wait()
        scores = [
            lax.dot_general(head.astype(BF), k_s[r], NT, preferred_element_type=F32) * scale
            for r, head in zip(requests, heads)
        ]
        expo = [jnp.where(position < len_s[r], jnp.exp(score), 0.0) for r, score in zip(requests, scores)]
        denom = [jnp.sum(e, axis=1, keepdims=True) + o for e, o in zip(expo, own)]
        weights += [(e / d).astype(BF) for e, d in zip(expo, denom)]
        own_weights += [(o / d).astype(BF).astype(F32) for o, d in zip(own, denom)]
    pl.semaphore_wait(barrier, len(plane) + NZ)
    up_here = fetch(up_ref, wu.at[core], w_loc.at[0])
    down_rows = pl.ds(pl.multiple_of(core * 128, 128), 128)
    down_other = pl.ds(pl.multiple_of(other * 128, 128), 128)
    send(up_ref, wu.at[core], w_send.at[0], w_recv.at[0], partner)
    for copy in small[3:]:
        copy.wait()
    vnf[...] = vn_s[...].astype(F32)
    for n in range(R // STEP):
        requests = range(n * STEP, (n + 1) * STEP)
        values_in[n].wait()
        mixed = [
            jnp.dot(weights[r], v_s[r], preferred_element_type=F32) + own_weights[r] * vnf[r : r + 1, :]
            for r in requests
        ]
        for r, part in zip(requests, mixed):
            att[r : r + 1, :] = jnp.sum(jnp.where(mine_head, part, 0.0), axis=0, keepdims=True)
    values = (resid_s[...].astype(F32) + att[...]).astype(BF).astype(F32)

    eye = (
        lax.broadcasted_iota(jnp.int32, (R, 128), 0) == lax.broadcasted_iota(jnp.int32, (R, 128), 1)
    ).astype(F32)
    own_mean = jnp.mean(values, axis=1, keepdims=True)
    off = values - own_mean
    own_sq = jnp.sum(off * off, axis=1, keepdims=True)
    here = stats.at[group(0, 0)]
    here[0:1, :] = jnp.sum(own_mean * eye, axis=0, keepdims=True)
    here[1:2, :] = jnp.sum(own_sq * eye, axis=0, keepdims=True)
    for n, (i, j) in enumerate(plane):
        send(here, here, st_send.at[n], st_recv.at[n], near(i, j))
    down_here = fetch(down_ref, wd.at[down_rows], w_loc.at[1])
    send(down_ref, wd.at[down_rows], w_send.at[1], w_recv.at[1], partner)

    block0 = z * 32 + group(0, 0)
    hit0 = jnp.max((active_s[...] == block0).astype(F32), axis=1, keepdims=True)
    hit1 = jnp.max((active_s[...] == block0 + 16).astype(F32), axis=1, keepdims=True)
    spans = active_s.shape[0]
    hits = jnp.concatenate([jnp.broadcast_to(hit0, (spans, 128)), jnp.broadcast_to(hit1, (spans, 128))], axis=1)
    row_at = lax.broadcasted_iota(jnp.int32, (ROWS, spans), 0)
    span_at = lax.broadcasted_iota(jnp.int32, (ROWS, spans), 1)
    lie = row_at // R
    away = jnp.where(lie % 2 == 1, (lie + 1) // 2, (NZ - lie // 2) % NZ)
    span_of = (((z + away) % NZ) * 2 + core) * 4 + (row_at % R) // 4
    row_mask = jnp.dot((span_of == span_at).astype(BF), hits.astype(BF), preferred_element_type=F32)
    gain = jnp.concatenate([gain_s[pl.ds(group(0, 0) * 6 + n, 1), :] for n in range(cols // 128)], axis=1)

    for n, (i, j) in enumerate(plane):
        arrived(stats.at[group(4 - i, 4 - j)], st_recv.at[n])
    means, squares = stats[:, 0, :], stats[:, 1, :]
    mean_all = jnp.sum(means, axis=0, keepdims=True) * (1.0 / 16)
    gap = means - mean_all
    var_all = (jnp.sum(squares, axis=0, keepdims=True) + cols * jnp.sum(gap * gap, axis=0, keepdims=True)) * (
        1.0 / width
    )
    mean_row = jnp.sum(mean_all * eye, axis=1, keepdims=True)
    rstd_row = jnp.sum(lax.rsqrt(var_all + 1e-05) * eye, axis=1, keepdims=True)
    mine = slot(0, 0)
    mine[0:R, :] = ((values - mean_row) * rstd_row * gain).astype(BF)

    def lies(k):
        return pl.ds(DIST.index(k) * R, R)

    for k in (1, 7, 6, 2, 5, 3, 4):
        send(mine.at[0:R], mine.at[lies(NZ - k)], z_send.at[k - 1], z_recv.at[k - 1], along_z(k))

    part_rows = [pl.ds(h * HALF, HALF) for h in range(2)]
    first = [pl.ds(h * HALF, QUART) for h in range(2)]
    second = [pl.ds(h * HALF + QUART, QUART) for h in range(2)]

    def copy1(j, rows, n, h, to):
        send(slot(0, j).at[rows], slot(0, j).at[rows], p1_send.at[n, h], p1_recv.at[n, h], near(0, to))

    def copy2(i, j, rows, n, h, to):
        send(slot(i, j).at[rows], slot(i, j).at[rows], p2_send.at[n, h, j], p2_recv.at[n, h, j], near(to, 0))

    def spread(j, h):
        copy2(0, j, part_rows[h], 0, h, 1)
        copy2(0, j, part_rows[h], 1, h, 3)

    def relay1(h):
        arrived(slot(0, 3).at[part_rows[h]], p1_recv.at[0, h])
        copy1(3, first[h], 2, h, 1)
        spread(3, h)
        arrived(slot(0, 1).at[part_rows[h]], p1_recv.at[1, h])
        copy1(1, second[h], 3, h, 3)
        spread(1, h)

    def opposite1(h):
        arrived(slot(0, 2).at[first[h]], p1_recv.at[2, h])
        arrived(slot(0, 2).at[second[h]], p1_recv.at[3, h])
        spread(2, h)

    def relay2(j, h):
        arrived(slot(3, j).at[part_rows[h]], p2_recv.at[0, h, j])
        copy2(3, j, first[h], 2, h, 1)
        arrived(slot(1, j).at[part_rows[h]], p2_recv.at[1, h, j])
        copy2(1, j, second[h], 3, h, 3)

    def opposite2(j, h):
        arrived(slot(2, j).at[first[h]], p2_recv.at[2, h, j])
        arrived(slot(2, j).at[second[h]], p2_recv.at[3, h, j])

    def up(i, j):
        rows = pl.ds(pl.multiple_of(group(i, j) * cols, 128), cols)
        both = jnp.concatenate([wu[0, rows, :], wu[1, rows, :]], axis=1)
        return jnp.dot(slot(i, j)[...], both, preferred_element_type=F32)

    for h, distances in enumerate(((1, 7, 2), (6, 3, 5, 4))):
        for k in distances:
            arrived(mine.at[lies(k)], z_recv.at[NZ - k - 1])
        copy1(0, part_rows[h], 0, h, 1)
        copy1(0, part_rows[h], 1, h, 3)
        spread(0, h)
    relay1(0)
    relay2(0, 0)
    relay1(1)
    opposite1(0)
    relay2(0, 1)
    opposite1(1)
    relay2(3, 0)
    relay2(1, 0)
    up_here.wait()
    arrived(wu.at[other], w_recv.at[0])
    before = up(0, 0) + up(0, 3) + up(0, 1) + up(0, 2)
    relay2(3, 1)
    before += up(3, 0) + up(1, 0)
    relay2(1, 1)
    before += up(3, 3) + up(1, 3)
    relay2(2, 0)
    before += up(3, 1) + up(1, 1)
    relay2(2, 1)
    before += up(3, 2) + up(1, 2)
    for j in (0, 3, 1, 2):
        opposite2(j, 0)
        opposite2(j, 1)
        before += up(2, j)
    hidden = (jnp.maximum(before, 0.0) * row_mask).astype(BF)

    down_here.wait()
    arrived(wd.at[down_other], w_recv.at[1])
    back = (2, 3, 1, 0)

    def down(i, j, h):
        columns = pl.ds(pl.multiple_of(group(i, j) * cols, 128), cols)
        return jnp.dot(hidden[h * HALF : (h + 1) * HALF], wd[:, columns], preferred_element_type=F32)

    for h in (1, 0):
        for j in back:
            ya[j, part_rows[h], :] = down(2, j, h).astype(BF)
            send(ya.at[j, first[h]], ra.at[j, first[h]], a_send.at[0, h, j], a_recv.at[0, h, j], near(1, 0))
            send(ya.at[j, second[h]], ra.at[j, second[h]], a_send.at[1, h, j], a_recv.at[1, h, j], near(3, 0))
    for h in (1, 0):
        for j in back:
            part = down(1, j, h)
            arrived(ra.at[j, first[h]], a_recv.at[0, h, j])
            yr[j, first[h], :] = (part[:QUART] + ra[j, first[h], :].astype(F32)).astype(BF)
            yr[j, second[h], :] = part[QUART:].astype(BF)
            send(yr.at[j, part_rows[h]], rl.at[j, part_rows[h]], b_send.at[0, h, j], b_recv.at[0, h, j], near(1, 0))
            part = down(3, j, h)
            arrived(ra.at[j, second[h]], a_recv.at[1, h, j])
            yl[j, first[h], :] = part[:QUART].astype(BF)
            yl[j, second[h], :] = (part[QUART:] + ra[j, second[h], :].astype(F32)).astype(BF)
            send(yl.at[j, part_rows[h]], rr.at[j, part_rows[h]], b_send.at[1, h, j], b_recv.at[1, h, j], near(3, 0))

    def settled(j, h):
        part = down(0, j, h)
        arrived(rl.at[j, part_rows[h]], b_recv.at[0, h, j])
        part += rl[j, part_rows[h], :].astype(F32)
        arrived(rr.at[j, part_rows[h]], b_recv.at[1, h, j])
        return part + rr[j, part_rows[h], :].astype(F32)

    def settle_opposite(h):
        pa[part_rows[h], :] = settled(2, h).astype(BF)
        send(pa.at[first[h]], qa.at[first[h]], c_send.at[0, h], c_recv.at[0, h], near(0, 1))
        send(pa.at[second[h]], qa.at[second[h]], c_send.at[1, h], c_recv.at[1, h], near(0, 3))

    def settle_beside(h):
        part = settled(3, h)
        arrived(qa.at[second[h]], c_recv.at[1, h])
        pleft[first[h], :] = part[:QUART].astype(BF)
        pleft[second[h], :] = (part[QUART:] + qa[second[h], :].astype(F32)).astype(BF)
        send(pleft.at[part_rows[h]], qr.at[part_rows[h]], c_send.at[3, h], c_recv.at[3, h], near(0, 3))
        part = settled(1, h)
        arrived(qa.at[first[h]], c_recv.at[0, h])
        pr[first[h], :] = (part[:QUART] + qa[first[h], :].astype(F32)).astype(BF)
        pr[second[h], :] = part[QUART:].astype(BF)
        send(pr.at[part_rows[h]], ql.at[part_rows[h]], c_send.at[2, h], c_recv.at[2, h], near(0, 1))

    def settle_own(h, distances):
        part = settled(0, h)
        arrived(ql.at[part_rows[h]], c_recv.at[2, h])
        part += ql[part_rows[h], :].astype(F32)
        arrived(qr.at[part_rows[h]], c_recv.at[3, h])
        part += qr[part_rows[h], :].astype(F32)
        tz[part_rows[h], :] = part.astype(BF)
        for k in distances:
            send(tz.at[lies(k)], rz.at[k - 1], zz_send.at[k - 1], zz_recv.at[k - 1], along_z(k))
        return part

    settle_opposite(1)
    settle_beside(1)
    settle_opposite(0)
    settle_own(1, (4, 3, 5, 6))
    settle_beside(0)
    total = settle_own(0, (2, 1, 7))[:R] + values
    for k in (4, 3, 5, 6, 2, 1, 7):
        arrived(rz.at[k - 1], zz_recv.at[k - 1])
        total += rz[k - 1].astype(F32)
    out_ref[...] = total.astype(BF)
    for copy in started:
        copy.wait_send()


def layer(resid, query, key_new, value_new, key_cache, value_cache, lengths, norm_gain, active, up, down):
    cols = resid.shape[1]
    width = 16 * cols
    hbm = pl.BlockSpec(memory_space=pl.ANY)
    dma = pltpu.SemaphoreType.DMA
    row = pltpu.VMEM((R, cols), BF)
    row32 = pltpu.VMEM((R, cols), F32)
    cache = pltpu.VMEM((R, 128, cols), BF)
    full = pltpu.VMEM((ROWS, cols), BF)
    four = pltpu.VMEM((4, ROWS, cols), BF)
    return pl.pallas_call(
        layer_kernel,
        out_shape=jax.ShapeDtypeStruct((R, cols), BF),
        in_specs=[hbm] * 11,
        out_specs=pl.BlockSpec(memory_space=pltpu.VMEM),
        scratch_shapes=[
            row, row, row, row, cache, cache,
            pltpu.SMEM((R,), jnp.int32),
            pltpu.VMEM((norm_gain.shape[0] // 128, 128), F32),
            pltpu.VMEM(active.shape, jnp.int32),
            row32, row32, row32, row32,
            pltpu.VMEM((4, 4, ROWS, cols), BF),
            pltpu.VMEM((2, width, 128), BF),
            pltpu.VMEM((256, width), BF),
            pltpu.VMEM((16, 2, 128), F32),
            four, four, four, four, four, four,
            full, full, full, full, full, full, full,
            pltpu.VMEM((NZ - 1, R, cols), BF),
            dma((7,)), dma((R // STEP,)), dma((R // STEP,)),
            dma((2,)), dma((2,)), dma((2,)),
            dma((15,)), dma((15,)),
            dma((NZ - 1,)), dma((NZ - 1,)),
            dma((4, 2)), dma((4, 2)),
            dma((4, 2, 4)), dma((4, 2, 4)),
            dma((2, 2, 4)), dma((2, 2, 4)), dma((2, 2, 4)), dma((2, 2, 4)),
            dma((4, 2)), dma((4, 2)),
            dma((NZ - 1,)), dma((NZ - 1,)),
        ],
        compiler_params=pltpu.CompilerParams(
            collective_id=0, has_side_effects=True, vmem_limit_bytes=60 * 1024 * 1024
        ),
        name="layer",
    )(resid, query, key_new, value_new, key_cache, value_cache, lengths, norm_gain.reshape(-1, 128), active, up, down)


def shards(
    resid, query, key_new, value_new, key_cache, value_cache, lengths, norm_gain, active, up_weight, down_weight
):
    return layer(
        resid, query, key_new, value_new, key_cache, value_cache, lengths, norm_gain, active, up_weight, down_weight
    )


def solution(mesh):
    placed = (
        P("attn", ("ffn", "grp")),
        P("attn", ("ffn", "grp")),
        P("attn", ("ffn", "grp")),
        P("attn", ("ffn", "grp")),
        P("attn", None, ("ffn", "grp")),
        P("attn", None, ("ffn", "grp")),
        P("attn"),
        P(),
        P(),
        P(None, ("attn", "ffn", "grp")),
        P(("attn", "ffn", "grp"), None),
    )
    return jax.shard_map(
        shards, mesh=mesh, in_specs=placed, out_specs=P("attn", ("ffn", "grp")), check_vma=False
    )
```

time: 90.4 us -> 70.2 us (0.78)
  Pallas kernels: 79.7 us -> 68.7 us
  local copies, waits for them, and re-layouts: 9.96 us -> 1.35 us
    pallas_call x2 -> x1, Pallas kernels: 79.7 us -> 68.7 us  [layer(): pl.pallas_call(layer_kernel, out_shape=jax.ShapeDtypeStruct((R, cols), BF...]
    unnamed x19 -> x1, local copies, waits for them, and re-layouts: 9.33 us -> 1.35 us
where the time goes in v2:
time: 70.2 us; the launch traced here: 70.1 us
  Pallas kernels  68.7 us (98%)
  local copies, waits for them, and re-layouts  1.35 us (2%)
    pallas_call x1, Pallas kernels, layer(): pl.pallas_call(layer_kernel, out_shape=jax.ShapeDtypeStruct((R, cols), BF...  68.7 us

profile of v2, /device:TPU:2, one launch (start us, length us, event | category | flops | bytes accessed | tf_op | source)
XLA Modules:
  0.0 70.1 jit_solution(15421825480074512061)
XLA Ops:
  0.0 68.7 %layer.1 = bf16[16,768]{1,0:T(8,128)(2,1)} custom-call(bf16[16,768]{1,0:T(8,128)(2,1)} %resid_ref.1, bf16[16,768]{1,0:T(8,128)(2,1)} %q_ref.1, bf16[16,768]{1,0:T(8,128)(2,1)} %kn_ref.1, bf16[16,768]{1,0:T(8,128)(2,1)} %vn_ref.1, bf16[16,128,768]{2,1,0:T(8,128)(2,1)} %k_ref.1, bf16[16,128,768]{2,1,0:T(8,128)(2,1)} %v_ref.1, s32[16]{0:T(128)} %len_ref.1, ...), custom_call_target="tpu_custom_call" | custom-call | tf_op jit(solution)/shard_map/layer/pallas_call | solution.py:343
  68.7 1.3 %copy.13 = bf16[16,768]{1,0:T(8,128)(2,1)} copy(bf16[16,768]{1,0:T(8,128)(2,1)} %layer.1) | data formatting | bytes 49152

commit v3 on v2

v3 whole, which is shorter than its diff:
```python
import jax
import jax.numpy as jnp
from jax import lax
from jax.experimental import pallas as pl
from jax.experimental.pallas import tpu as pltpu
from jax.sharding import PartitionSpec as P

MESH = pl.DeviceIdType.MESH
HD = 128
BF = jnp.bfloat16
F32 = jnp.float32
NT = (((1,), (1,)), ((), ()))
R = 16
NZ = 8
ROWS = R * NZ
DIST = (0, 1, 7, 2, 6, 3, 5, 4)
STEP = 4
CB = 128
CHUNKS = (slice(0, 16), slice(16, 64), slice(64, 128))


def layer_kernel(
    resid_ref, q_ref, kn_ref, vn_ref, k_ref, v_ref, len_ref, gain_ref, active_ref, up_ref, down_ref, out_ref,
    resid_s, q_s, kn_s, vn_s, k_s, v_s, len_s, gain_s, active_s, qf, knf, vnf, att,
    xbuf, wu, wd, stats,
    gb, us, zst, yf, ya, yr, yl, ra, rlr, ps, qs, tz, rz, xb, pb, zs, zr, tb, rxy,
    in_sem, k_sem, v_sem, w_loc, w_send, w_recv, st_send, st_recv, sz_send, sz_recv, z_send, z_recv, p1_send, p1_recv, p2_send, p2_recv, p2o_recv,
    a_send, a_recv, b_send, b_recv, c_send, c_recv, zz_send, zz_recv,
    xy_send, xy_recv, ring_send, ring_recv, back_send, back_recv, xyb_send, xyb_recv,
):
    attn, ffn, grp = lax.axis_index("attn"), lax.axis_index("ffn"), lax.axis_index("grp")
    z, core = attn // 2, attn % 2
    x, y = ffn // 2, (ffn % 2) * 2 + grp
    other = 1 - core
    p1 = x * other + y * core
    p2 = y * other + x * core
    cols = resid_ref.shape[1]
    ca = cols - CB
    width = 16 * cols

    def place(z_at, core_at, x_at, y_at):
        return (z_at * 2 + core_at, x_at * 2 + y_at // 2, y_at % 2)

    def near(i, j):
        q2, q1 = (p2 + i) % 4, (p1 + j) % 4
        return place(z, core, q1 * other + q2 * core, q2 * other + q1 * core)

    def along_z(k):
        return place((z + k) % NZ, core, x, y)

    def group(i, j):
        q2, q1 = (p2 + i) % 4, (p1 + j) % 4
        return (q1 * other + q2 * core) * 4 + q2 * other + q1 * core

    def slot(i, j):
        return xbuf.at[(p2 + i) % 4, (p1 + j) % 4]

    def send(src, dst, s_sem, r_sem, device):
        copy = pltpu.make_async_remote_copy(
            src_ref=src, dst_ref=dst, send_sem=s_sem, recv_sem=r_sem, device_id=device, device_id_type=MESH
        )
        copy.start()

    def sent(src, s_sem):
        pltpu.make_async_remote_copy(
            src_ref=src, dst_ref=src, send_sem=s_sem, recv_sem=s_sem, device_id=near(0, 1), device_id_type=MESH
        ).wait_send()

    def arrived(dst, r_sem):
        pltpu.make_async_remote_copy(
            src_ref=dst, dst_ref=dst, send_sem=r_sem, recv_sem=r_sem, device_id=near(0, 1), device_id_type=MESH
        ).wait_recv()

    def fetch(src, dst, sem):
        copy = pltpu.make_async_copy(src, dst, sem)
        copy.start()
        return copy

    small = [
        fetch(src, dst, in_sem.at[n])
        for n, (src, dst) in enumerate(
            [(q_ref, q_s), (kn_ref, kn_s), (len_ref, len_s), (vn_ref, vn_s), (resid_ref, resid_s),
             (gain_ref, gain_s), (active_ref, active_s)]
        )
    ]
    steps = [pl.ds(n * STEP, STEP) for n in range(R // STEP)]
    keys_in = [fetch(k_ref.at[rows], k_s.at[rows], k_sem.at[n]) for n, rows in enumerate(steps)]
    values_in = [fetch(v_ref.at[rows], v_s.at[rows], v_sem.at[n]) for n, rows in enumerate(steps)]

    plane = [(i, j) for i in range(4) for j in range(4) if (i, j) != (0, 0)]
    barrier = pltpu.get_barrier_semaphore()
    partner = place(z, other, x, y)
    for i, j in plane:
        pl.semaphore_signal(barrier, inc=1, device_id=near(i, j), device_id_type=MESH)
    for k in range(1, NZ):
        pl.semaphore_signal(barrier, inc=1, device_id=along_z(k), device_id_type=MESH)
    pl.semaphore_signal(barrier, inc=1, device_id=partner, device_id_type=MESH)

    scale = HD ** (-0.5)
    head_of = lax.broadcasted_iota(jnp.int32, (8, cols), 1) // HD
    mine_head = head_of == lax.broadcasted_iota(jnp.int32, (8, cols), 0)
    position = lax.broadcasted_iota(jnp.int32, (8, HD), 1)
    for copy in small[:3]:
        copy.wait()
    qf[...] = q_s[...].astype(F32)
    knf[...] = kn_s[...].astype(F32)
    weights, own_weights = [], []
    for n in range(R // STEP):
        requests = range(n * STEP, (n + 1) * STEP)
        heads = [jnp.where(mine_head, qf[r : r + 1, :], 0.0) for r in requests]
        own = [
            jnp.exp(jnp.sum(head * knf[r : r + 1, :], axis=1, keepdims=True) * scale)
            for r, head in zip(requests, heads)
        ]
        keys_in[n].wait()
        scores = [
            lax.dot_general(head.astype(BF), k_s[r], NT, preferred_element_type=F32) * scale
            for r, head in zip(requests, heads)
        ]
        expo = [jnp.where(position < len_s[r], jnp.exp(score), 0.0) for r, score in zip(requests, scores)]
        denom = [jnp.sum(e, axis=1, keepdims=True) + o for e, o in zip(expo, own)]
        weights += [(e / d).astype(BF) for e, d in zip(expo, denom)]
        own_weights += [(o / d).astype(BF).astype(F32) for o, d in zip(own, denom)]
    pl.semaphore_wait(barrier, len(plane) + NZ)
    up_here = fetch(up_ref, wu.at[core], w_loc.at[0])
    down_rows = pl.ds(pl.multiple_of(core * 128, 128), 128)
    down_other = pl.ds(pl.multiple_of(other * 128, 128), 128)
    send(up_ref, wu.at[core], w_send.at[0], w_recv.at[0], partner)
    for copy in small[3:]:
        copy.wait()
    vnf[...] = vn_s[...].astype(F32)
    for n in range(R // STEP):
        requests = range(n * STEP, (n + 1) * STEP)
        values_in[n].wait()
        mixed = [
            jnp.dot(weights[r], v_s[r], preferred_element_type=F32) + own_weights[r] * vnf[r : r + 1, :]
            for r in requests
        ]
        for r, part in zip(requests, mixed):
            att[r : r + 1, :] = jnp.sum(jnp.where(mine_head, part, 0.0), axis=0, keepdims=True)
    values = (resid_s[...].astype(F32) + att[...]).astype(BF).astype(F32)

    def lies(k):
        return pl.ds(DIST.index(k) * R, R)

    gain = jnp.concatenate([gain_s[pl.ds(group(0, 0) * 6 + n, 1), :] for n in range(cols // 128)], axis=1)
    own_mean = jnp.mean(values, axis=1, keepdims=True)
    off = values - own_mean
    scaled = (off * gain).astype(BF)
    mine = slot(0, 0)
    mine[0:R, :] = scaled[:, :ca]
    mine_b = xb.at[0, p2 * 4 + p1]
    mine_b[...] = scaled[:, ca:]

    def copy1(t, c):
        rows = CHUNKS[c]
        send(slot(0, 0).at[rows], slot(0, 0).at[rows], p1_send, p1_recv.at[t - 1, c], near(0, t))

    def copy2(i, j, rows, n, c, to):
        if rows.start < rows.stop:
            sem = p2_recv.at[n, c, j] if n < 2 else p2o_recv.at[j]
            send(slot(i, j).at[rows], slot(i, j).at[rows], p2_send, sem, near(to, 0))

    def spread(j, c):
        copy2(0, j, CHUNKS[c], 0, c, 1)
        copy2(0, j, CHUNKS[c], 1, c, 3)

    def own_part(c):
        for t in (1, 3, 2):
            copy1(t, c)
        spread(0, c)

    def to_z(distances):
        for k in distances:
            send(mine.at[0:R], mine.at[lies(NZ - k)], z_send, z_recv.at[0 if k in (1, 7, 6) else 1], along_z(k))

    to_z((1, 7, 6))
    own_part(0)
    to_z((2, 5, 3, 4))
    for i, j in plane:
        send(mine_b, mine_b, xy_send, xy_recv, near(i, j))

    lane = lax.broadcasted_iota(jnp.int32, (R, 128), 1)
    line = lax.broadcasted_iota(jnp.int32, (R, 128), 0)
    g_here = group(0, 0)
    eye = (lane == (g_here % 8) * 16 + line).astype(F32)
    own_sq = jnp.sum(off * off, axis=1, keepdims=True)
    here = stats.at[g_here]
    here[0:1, :] = jnp.sum(own_mean * eye, axis=0, keepdims=True)
    here[1:2, :] = jnp.sum(own_sq * eye, axis=0, keepdims=True)
    for i, j in plane:
        send(here, here, st_send, st_recv, near(i, j))
    down_here = fetch(down_ref, wd.at[down_rows], w_loc.at[1])
    send(down_ref, wd.at[down_rows], w_send.at[1], w_recv.at[1], partner)

    for g in range(16):
        row = jnp.concatenate([gain_s[g * 6 + n : g * 6 + n + 1, :] for n in range(cols // 128)], axis=1)
        high = row.astype(BF).astype(F32)
        upper = lax.broadcasted_iota(jnp.int32, (16, cols), 0) < 8
        gb[g] = jnp.where(upper, high, row - high).astype(BF)

    block0 = z * 32 + group(0, 0)
    hit0 = jnp.max((active_s[...] == block0).astype(F32), axis=1, keepdims=True)
    hit1 = jnp.max((active_s[...] == block0 + 16).astype(F32), axis=1, keepdims=True)
    spans = active_s.shape[0]
    hits = jnp.concatenate([jnp.broadcast_to(hit0, (spans, 128)), jnp.broadcast_to(hit1, (spans, 128))], axis=1)
    row_at = lax.broadcasted_iota(jnp.int32, (ROWS, spans), 0)
    span_at = lax.broadcasted_iota(jnp.int32, (ROWS, spans), 1)
    lie = row_at // R
    away = jnp.where(lie % 2 == 1, (lie + 1) // 2, (NZ - lie // 2) % NZ)
    span_of = (((z + away) % NZ) * 2 + core) * 4 + (row_at % R) // 4
    row_mask = jnp.dot((span_of == span_at).astype(BF), hits.astype(BF), preferred_element_type=F32)
    def by_right(j, c):
        return (slice(0, 16 - 16 * (j % 2)), slice(16, 32 + 16 * (j % 2)), slice(64, 96))[c]

    def by_left(j, c):
        return (slice(16 - 16 * (j % 2), 16), slice(32 + 16 * (j % 2), 64), slice(96, 128))[c]

    def relay1(c):
        for j in (3, 1, 2):
            arrived(slot(0, j).at[CHUNKS[c]], p1_recv.at[3 - j, c])
            spread(j, c)

    def relay2(j, c):
        arrived(slot(3, j).at[CHUNKS[c]], p2_recv.at[0, c, j])
        copy2(3, j, by_right(j, c), 2, c, 1)
        arrived(slot(1, j).at[CHUNKS[c]], p2_recv.at[1, c, j])
        copy2(1, j, by_left(j, c), 3, c, 3)

    def opposite2(j):
        arrived(slot(2, j), p2o_recv.at[j])

    def up(i, j):
        g = group(i, j)
        rows = pl.ds(pl.multiple_of(g * cols, 128), ca)
        both = jnp.concatenate([wu[0, rows, :], wu[1, rows, :]], axis=1)
        lines = jnp.concatenate([slot(i, j)[...], gb[g, :, :ca]], axis=0)
        part = jnp.dot(lines, both, preferred_element_type=F32)
        us[g] = part[ROWS:]
        return part[:ROWS]

    pieces = [slice(0, 8), slice(8, 16)]

    def ring_on(way, step, piece):
        at, to = ((NZ - step) % NZ, NZ - step - 1) if way == 0 else (step, step + 1)
        send(
            xb.at[at, pieces[piece]], xb.at[to, pieces[piece]],
            ring_send, ring_recv.at[way, step, piece], along_z(1 if way == 0 else NZ - 1),
        )

    def ring_in(way, step, piece):
        at = NZ - step if way == 0 else step
        arrived(xb.at[at, pieces[piece]], ring_recv.at[way, step - 1, piece])

    def ring_start():
        arrived(xb.at[0, 0:15], xy_recv)
        for piece in range(2):
            for way in range(2):
                ring_on(way, 0, piece)

    def ring_relay(step, piece):
        for way in range(2):
            ring_in(way, step, piece)
            if step < 3 or piece == way:
                ring_on(way, step, piece)

    def ring_end():
        ring_in(0, 4, 0)
        ring_in(1, 4, 1)

    def up_b(q2, q1):
        g = (q1 * other + q2 * core) * 4 + q2 * other + q1 * core
        rows = pl.ds(pl.multiple_of(g * cols + ca, 128), CB)
        both = jnp.concatenate([wu[0, rows, :], wu[1, rows, :]], axis=1)
        lines = jnp.concatenate([xb[k, q2 * 4 + q1] for k in DIST] + [gb[g, :, ca:]], axis=0)
        part = jnp.dot(lines, both, preferred_element_type=F32)
        us[g] = us[g] + part[ROWS:]
        return part[:ROWS]

    relay1(0)
    arrived(mine.at[CHUNKS[1]], z_recv.at[0])
    own_part(1)
    ring_start()
    arrived(mine.at[CHUNKS[2]], z_recv.at[1])
    own_part(2)
    relay2(0, 0)
    relay1(1)
    ring_relay(1, 0)
    arrived(stats.at[0:15], st_recv)
    for half in range(2):
        zst[0, 2 * half : 2 * half + 2, :] = jnp.sum(stats[8 * half : 8 * half + 8], axis=0)
    for k in range(1, NZ):
        send(zst.at[0], zst.at[NZ - k], sz_send, sz_recv, along_z(k))
    ring_relay(1, 1)
    relay2(3, 0)
    relay2(1, 0)
    relay2(2, 0)
    relay1(2)
    relay2(0, 1)
    ring_relay(2, 0)
    relay2(3, 1)
    relay2(1, 1)
    ring_relay(2, 1)
    relay2(2, 1)
    relay2(0, 2)
    up_here.wait()
    arrived(wu.at[other], w_recv.at[0])
    before = up(0, 0) + up(0, 3)
    ring_relay(3, 0)
    relay2(3, 2)
    before += up(0, 1) + up(0, 2)
    ring_relay(3, 1)
    relay2(1, 2)
    before += up(3, 0) + up(1, 0)
    relay2(2, 2)
    before += up(3, 3) + up(1, 3)
    before += up(3, 1) + up(1, 1)
    before += up(3, 2) + up(1, 2)

    arrived(zst.at[1:NZ], sz_recv)
    own_lane = lane % 16 == line
    mean_at, square_at = [
        [jnp.concatenate([jnp.where(own_lane, zst[k, 2 * half + n : 2 * half + n + 1, :], 0.0) for k in DIST], axis=0) for half in range(2)]
        for n in range(2)
    ]
    mean_row = jnp.sum(mean_at[0] + mean_at[1], axis=1, keepdims=True) * (1.0 / 16)
    lanes = lax.broadcasted_iota(jnp.int32, (ROWS, 128), 1) % 16 == lax.broadcasted_iota(jnp.int32, (ROWS, 128), 0) % 16
    gaps = [jnp.where(lanes, part - mean_row, 0.0) for part in mean_at]
    var_row = jnp.sum(
        square_at[0] + square_at[1] + cols * (gaps[0] * gaps[0] + gaps[1] * gaps[1]), axis=1, keepdims=True
    ) * (1.0 / width)
    rstd_row = lax.rsqrt(var_row + 1e-05)

    for j in (0, 3, 1, 2):
        opposite2(j)
        before += up(2, j)
    ring_end()
    for q2 in range(4):
        for q1 in range(4):
            before += up_b(q2, q1)
    for half in range(2):
        gains = []
        for g in range(8 * half, 8 * half + 8):
            both = us[g, :8, :] + us[g, 8:, :]
            gains += [both, both]
        before += jnp.dot(
            gaps[half], jnp.concatenate(gains, axis=0), preferred_element_type=F32, precision=lax.Precision.HIGHEST
        )
    hidden = (jnp.maximum(before * rstd_row, 0.0) * row_mask).astype(BF)

    down_here.wait()
    arrived(wd.at[down_other], w_recv.at[1])
    back = (2, 3, 1, 0)

    def down(i, j):
        columns = pl.ds(pl.multiple_of(group(i, j) * cols, 128), ca)
        return jnp.dot(hidden, wd[:, columns], preferred_element_type=F32)

    def pass_on(src, dst, j, rows, c, to, s_sem, r_sem):
        if rows.start < rows.stop:
            send(src.at[j, rows], dst.at[j, rows], s_sem, r_sem.at[c, j], near(to, 0))

    def with_arrived(base, j, rows, out):
        if rows.start < rows.stop:
            out[j, rows, :] = (yf[base, j, rows, :] + ra[j, rows, :].astype(F32)).astype(BF)

    def alone(base, j, rows, out):
        if rows.start < rows.stop:
            out[j, rows, :] = yf[base, j, rows, :].astype(BF)

    def start_back(c):
        for j in back:
            pass_on(ya, ra, j, by_right(j, c), c, 1, a_send, a_recv)
            pass_on(ya, ra, j, by_left(j, c), c, 3, a_send, a_recv)

    def beside_back(j, c):
        alone(0, j, by_left(j, c), yr)
        alone(1, j, by_right(j, c), yl)
        arrived(ra.at[j, CHUNKS[c]], a_recv.at[c, j])
        with_arrived(0, j, by_right(j, c), yr)
        pass_on(yr, rlr.at[0], j, CHUNKS[c], c, 1, b_send.at[0], b_recv)
        with_arrived(1, j, by_left(j, c), yl)
        pass_on(yl, rlr.at[1], j, CHUNKS[c], c, 3, b_send.at[1], b_recv)

    def ring_back(way, k, piece):
        away = k if way == 0 else NZ - k
        part = pb[away, pieces[piece]]
        if k < 3 or (k == 3 and piece == way):
            arrived(zr.at[way, k, pieces[piece]], back_recv.at[way, k, piece])
            part += zr[way, k, pieces[piece]].astype(F32)
        zs[way, k - 1, pieces[piece]] = part.astype(BF)
        send(
            zs.at[way, k - 1, pieces[piece]], zr.at[way, k - 1, pieces[piece]],
            back_send, back_recv.at[way, k - 1, piece], along_z(1 if way == 0 else NZ - 1),
        )

    for j in back:
        ya[j] = down(2, j).astype(BF)
    start_back(2)
    for q2 in range(4):
        for q1 in range(4):
            g = (q1 * other + q2 * core) * 4 + q2 * other + q1 * core
            columns = pl.ds(pl.multiple_of(g * cols + ca, 128), CB)
            part = jnp.dot(hidden, wd[:, columns], preferred_element_type=F32)
            for n, k in enumerate(DIST):
                pb[k, q2 * 4 + q1] = part[n * R : (n + 1) * R]
    ring_back(0, 4, 0)
    ring_back(1, 4, 1)
    ring_back(0, 3, 1)
    ring_back(1, 3, 0)
    start_back(1)
    start_back(0)
    for j in back:
        yf[0, j] = down(1, j)
        yf[1, j] = down(3, j)
        beside_back(j, 2)
    ring_back(0, 3, 0)
    ring_back(1, 3, 1)
    for j in back:
        beside_back(j, 1)
    ring_back(0, 2, 1)
    ring_back(1, 2, 0)
    for j in back:
        beside_back(j, 0)
    ring_back(0, 2, 0)
    ring_back(1, 2, 1)
    for j in back:
        yf[2, j] = down(0, j)

    def settled(j, c):
        rows = CHUNKS[c]
        arrived(rlr.at[:, j, rows], b_recv.at[c, j])
        return yf[2, j, rows, :] + rlr[0, j, rows, :].astype(F32) + rlr[1, j, rows, :].astype(F32)

    def settle(c):
        rows = CHUNKS[c]
        for j in (2, 3, 1):
            ps[j - 1, rows, :] = settled(j, c).astype(BF)
            send(ps.at[j - 1, rows], qs.at[j - 1, rows], c_send, c_recv.at[c], near(0, j))

    def settle_own(c):
        rows = CHUNKS[c]
        part = settled(0, c)
        arrived(qs.at[:, rows], c_recv.at[c])
        for j in (3, 1, 2):
            part += qs[j - 1, rows, :].astype(F32)
        return part

    def to_owners(c, distances):
        rows = CHUNKS[c]
        tz[rows, :] = settle_own(c).astype(BF)
        for k in distances:
            send(tz.at[lies(k)], rz.at[k - 1], zz_send, zz_recv, along_z(k))

    settle(2)
    ring_back(0, 1, 1)
    ring_back(1, 1, 0)
    settle(1)
    to_owners(2, (4, 3, 5, 6))
    ring_back(0, 1, 0)
    ring_back(1, 1, 1)
    settle(0)
    to_owners(1, (2, 1, 7))
    for piece in range(2):
        for way in range(2):
            arrived(zr.at[way, 0, pieces[piece]], back_recv.at[way, 0, piece])
    whole = pb[0] + zr[0, 0].astype(F32) + zr[1, 0].astype(F32)
    pb[0] = whole
    tb[...] = whole.astype(BF)
    for n, (i, j) in enumerate(plane):
        send(tb.at[(p2 + i) % 4 * 4 + (p1 + j) % 4], rxy.at[n], xyb_send, xyb_recv, near(i, j))
    total = settle_own(0) + values[:, :ca]
    total_b = pb[0, p2 * 4 + p1] + values[:, ca:]
    arrived(rz, zz_recv)
    for k in range(1, NZ):
        total += rz[k - 1].astype(F32)
    out_ref[:, :ca] = total.astype(BF)
    arrived(rxy, xyb_recv)
    for n in range(len(plane)):
        total_b += rxy[n].astype(F32)
    out_ref[:, ca:] = total_b.astype(BF)
    for src, sem in (
        (up_ref, w_send.at[0]), (down_ref, w_send.at[1]), (stats.at[0:15], st_send), (zst.at[1:NZ], sz_send),
        (mine.at[0 : ROWS - R], z_send), (xbuf.at[0, 0:3], p1_send), (xbuf.at[0:3], p2_send), (xb.at[0, 0:15], xy_send),
        (xb.at[0:7], ring_send), (xb.at[0:7], back_send), (ya, a_send), (yr, b_send.at[0]), (yl, b_send.at[1]),
        (ps, c_send), (rz, zz_send), (rxy, xyb_send),
    ):
        sent(src, sem)


def layer(resid, query, key_new, value_new, key_cache, value_cache, lengths, norm_gain, active, up, down):
    cols = resid.shape[1]
    width = 16 * cols
    hbm = pl.BlockSpec(memory_space=pl.ANY)
    dma = pltpu.SemaphoreType.DMA
    row = pltpu.VMEM((R, cols), BF)
    row32 = pltpu.VMEM((R, cols), F32)
    cache = pltpu.VMEM((R, 128, cols), BF)
    ca = cols - CB
    full = pltpu.VMEM((ROWS, ca), BF)
    four = pltpu.VMEM((4, ROWS, ca), BF)
    ring = (16, R, CB)
    one = dma(())
    return pl.pallas_call(
        layer_kernel,
        out_shape=jax.ShapeDtypeStruct((R, cols), BF),
        in_specs=[hbm] * 11,
        out_specs=pl.BlockSpec(memory_space=pltpu.VMEM),
        scratch_shapes=[
            row, row, row, row, cache, cache,
            pltpu.SMEM((R,), jnp.int32),
            pltpu.VMEM((norm_gain.shape[0] // 128, 128), F32),
            pltpu.VMEM(active.shape, jnp.int32),
            row32, row32, row32, row32,
            pltpu.VMEM((4, 4, ROWS, ca), BF),
            pltpu.VMEM((2, width, 128), BF),
            pltpu.VMEM((256, width), BF),
            pltpu.VMEM((16, 2, 128), F32),
            pltpu.VMEM((16, 16, cols), BF),
            pltpu.VMEM((16, 16, 256), F32),
            pltpu.VMEM((NZ, 4, 128), F32),
            pltpu.VMEM((3, 4, ROWS, ca), F32),
            four, four, four, four,
            pltpu.VMEM((2, 4, ROWS, ca), BF),
            pltpu.VMEM((3, ROWS, ca), BF),
            pltpu.VMEM((3, ROWS, ca), BF),
            full,
            pltpu.VMEM((NZ - 1, R, ca), BF),
            pltpu.VMEM((NZ,) + ring, BF),
            pltpu.VMEM((NZ,) + ring, F32),
            pltpu.VMEM((2, 4) + ring, BF),
            pltpu.VMEM((2, 4) + ring, BF),
            pltpu.VMEM(ring, BF),
            pltpu.VMEM((15, R, CB), BF),
            dma((7,)), dma((R // STEP,)), dma((R // STEP,)), dma((2,)), dma((2,)), dma((2,)),
            one, one, one, one, one, dma((2,)),
            one, dma((3, 3)), one, dma((2, 3, 4)), dma((4,)),
            one, dma((3, 4)), dma((2,)), dma((3, 4)), one, dma((3,)), one, one,
            one, one, one, dma((2, 4, 2)), one, dma((2, 4, 2)), one, one,
        ],
        compiler_params=pltpu.CompilerParams(
            collective_id=0, has_side_effects=True, vmem_limit_bytes=60 * 1024 * 1024
        ),
        name="layer",
    )(resid, query, key_new, value_new, key_cache, value_cache, lengths, norm_gain.reshape(-1, 128), active, up, down)


def shards(
    resid, query, key_new, value_new, key_cache, value_cache, lengths, norm_gain, active, up_weight, down_weight
):
    return layer(
        resid, query, key_new, value_new, key_cache, value_cache, lengths, norm_gain, active, up_weight, down_weight
    )


def solution(mesh):
    placed = (
        P("attn", ("ffn", "grp")),
        P("attn", ("ffn", "grp")),
        P("attn", ("ffn", "grp")),
        P("attn", ("ffn", "grp")),
        P("attn", None, ("ffn", "grp")),
        P("attn", None, ("ffn", "grp")),
        P("attn"),
        P(),
        P(),
        P(None, ("attn", "ffn", "grp")),
        P(("attn", "ffn", "grp"), None),
    )
    return jax.shard_map(
        shards, mesh=mesh, in_specs=placed, out_specs=P("attn", ("ffn", "grp")), check_vma=False
    )
```

time: 70.2 us -> 63.8 us (0.909); the launches traced: 70.1 us -> 63 us
  Pallas kernels: 68.7 us -> 61.6 us
    pallas_call x1, Pallas kernels: 68.7 us -> 61.6 us  [layer(): pl.pallas_call(layer_kernel, out_shape=jax.ShapeDtypeStruct((R, cols), BF...]
where the time goes in v3:
time: 63.8 us; the launch traced here: 63 us
  Pallas kernels  61.6 us (97%)
  local copies, waits for them, and re-layouts  1.35 us (2%)
    pallas_call x1, Pallas kernels, layer(): pl.pallas_call(layer_kernel, out_shape=jax.ShapeDtypeStruct((R, cols), BF...  61.6 us
    unnamed x1, local copies, waits for them, and re-layouts  1.35 us

profile of v3, /device:TPU:2, one launch (start us, length us, event | category | flops | bytes accessed | tf_op | source)
XLA Modules:
  0.0 63.0 jit_solution(3672181091196856687)
XLA Ops:
  0.0 61.6 %layer.1 = bf16[16,768]{1,0:T(8,128)(2,1)} custom-call(bf16[16,768]{1,0:T(8,128)(2,1)} %resid_ref.1, bf16[16,768]{1,0:T(8,128)(2,1)} %q_ref.1, bf16[16,768]{1,0:T(8,128)(2,1)} %kn_ref.1, bf16[16,768]{1,0:T(8,128)(2,1)} %vn_ref.1, bf16[16,128,768]{2,1,0:T(8,128)(2,1)} %k_ref.1, bf16[16,128,768]{2,1,0:T(8,128)(2,1)} %v_ref.1, s32[16]{0:T(128)} %len_ref.1, ...), custom_call_target="tpu_custom_call" | custom-call | tf_op jit(solution)/shard_map/layer/pallas_call | solution.py:504
  61.6 1.3 %copy.13 = bf16[16,768]{1,0:T(8,128)(2,1)} copy(bf16[16,768]{1,0:T(8,128)(2,1)} %layer.1) | data formatting | bytes 49152

commit v4 on v2

v4 whole, which is shorter than its diff:
```python
import functools

import jax
import jax.numpy as jnp
from jax import lax
from jax.experimental import pallas as pl
from jax.experimental.pallas import tpu as pltpu
from jax.sharding import PartitionSpec as P

MESH = pl.DeviceIdType.MESH
HD = 128
BF = jnp.bfloat16
F32 = jnp.float32
NT = (((1,), (1,)), ((), ()))
R = 16
NZ = 8
ROWS = R * NZ
DIST = (0, 1, 7, 2, 6, 3, 5, 4)
STEP = 4
CBS = ((0, 0), (256, 384))
CB = max(CBS[0] + CBS[1])
CHUNKS = (slice(0, 16), slice(16, 80), slice(80, 128))


def layer_kernel(
    resid_ref, q_ref, kn_ref, vn_ref, k_ref, v_ref, len_ref, gain_ref, active_ref, up_ref, down_ref, out_ref,
    resid_s, q_s, kn_s, vn_s, k_s, v_s, len_s, gain_s, active_s, qf, knf, vnf, att,
    xbuf, wu, wd, stats,
    gb, us, zst, yf_s, ya_s, yr_s, yl_s, ra_s, rlr_s, ps_s, qs_s, tz_s, rz_s, xb_s, pb_s, zs_s, zr_s, tb_s, rxy_s,
    in_sem, k_sem, v_sem, w_loc, w_send, w_recv, st_send, st_recv, sz_send, sz_recv, z_send, z_recv, p1_send, p1_recv, p2_send, p2_recv, p2o_recv,
    a_send, a_recv, b_send, b_recv, c_send, c_recv, zz_send, zz_recv,
    xy_send, xy_recv, ring_send, ring_recv, back_send, back_recv, xyb_send, xyb_recv,
):
    attn, ffn, grp = lax.axis_index("attn"), lax.axis_index("ffn"), lax.axis_index("grp")
    z, core = attn // 2, attn % 2
    x, y = ffn // 2, (ffn % 2) * 2 + grp
    other = 1 - core
    p1 = x * other + y * core
    p2 = y * other + x * core
    cols = resid_ref.shape[1]
    width = 16 * cols

    def place(z_at, core_at, x_at, y_at):
        return (z_at * 2 + core_at, x_at * 2 + y_at // 2, y_at % 2)

    def near(i, j):
        q2, q1 = (p2 + i) % 4, (p1 + j) % 4
        return place(z, core, q1 * other + q2 * core, q2 * other + q1 * core)

    def along_z(k):
        return place((z + k) % NZ, core, x, y)

    def group(i, j):
        q2, q1 = (p2 + i) % 4, (p1 + j) % 4
        return (q1 * other + q2 * core) * 4 + q2 * other + q1 * core

    def send(src, dst, s_sem, r_sem, device):
        copy = pltpu.make_async_remote_copy(
            src_ref=src, dst_ref=dst, send_sem=s_sem, recv_sem=r_sem, device_id=device, device_id_type=MESH
        )
        copy.start()

    def sent(src, s_sem):
        pltpu.make_async_remote_copy(
            src_ref=src, dst_ref=src, send_sem=s_sem, recv_sem=s_sem, device_id=near(0, 1), device_id_type=MESH
        ).wait_send()

    def arrived(dst, r_sem):
        pltpu.make_async_remote_copy(
            src_ref=dst, dst_ref=dst, send_sem=r_sem, recv_sem=r_sem, device_id=near(0, 1), device_id_type=MESH
        ).wait_recv()

    def fetch(src, dst, sem):
        copy = pltpu.make_async_copy(src, dst, sem)
        copy.start()
        return copy

    small = [
        fetch(src, dst, in_sem.at[n])
        for n, (src, dst) in enumerate(
            [(q_ref, q_s), (kn_ref, kn_s), (len_ref, len_s), (vn_ref, vn_s), (resid_ref, resid_s),
             (gain_ref, gain_s), (active_ref, active_s)]
        )
    ]
    steps = [pl.ds(n * STEP, STEP) for n in range(R // STEP)]
    keys_in = [fetch(k_ref.at[rows], k_s.at[rows], k_sem.at[n]) for n, rows in enumerate(steps)]
    values_in = [fetch(v_ref.at[rows], v_s.at[rows], v_sem.at[n]) for n, rows in enumerate(steps)]

    plane = [(i, j) for i in range(4) for j in range(4) if (i, j) != (0, 0)]
    barrier = pltpu.get_barrier_semaphore()
    partner = place(z, other, x, y)
    for i, j in plane:
        pl.semaphore_signal(barrier, inc=1, device_id=near(i, j), device_id_type=MESH)
    for k in range(1, NZ):
        pl.semaphore_signal(barrier, inc=1, device_id=along_z(k), device_id_type=MESH)
    pl.semaphore_signal(barrier, inc=1, device_id=partner, device_id_type=MESH)

    scale = HD ** (-0.5)
    head_of = lax.broadcasted_iota(jnp.int32, (8, cols), 1) // HD
    mine_head = head_of == lax.broadcasted_iota(jnp.int32, (8, cols), 0)
    position = lax.broadcasted_iota(jnp.int32, (8, HD), 1)
    for copy in small[:3]:
        copy.wait()
    qf[...] = q_s[...].astype(F32)
    knf[...] = kn_s[...].astype(F32)
    weights, own_weights = [], []
    for n in range(R // STEP):
        requests = range(n * STEP, (n + 1) * STEP)
        heads = [jnp.where(mine_head, qf[r : r + 1, :], 0.0) for r in requests]
        own = [
            jnp.exp(jnp.sum(head * knf[r : r + 1, :], axis=1, keepdims=True) * scale)
            for r, head in zip(requests, heads)
        ]
        keys_in[n].wait()
        scores = [
            lax.dot_general(head.astype(BF), k_s[r], NT, preferred_element_type=F32) * scale
            for r, head in zip(requests, heads)
        ]
        expo = [jnp.where(position < len_s[r], jnp.exp(score), 0.0) for r, score in zip(requests, scores)]
        denom = [jnp.sum(e, axis=1, keepdims=True) + o for e, o in zip(expo, own)]
        weights += [(e / d).astype(BF) for e, d in zip(expo, denom)]
        own_weights += [(o / d).astype(BF).astype(F32) for o, d in zip(own, denom)]
    pl.semaphore_wait(barrier, len(plane) + NZ)
    up_here = fetch(up_ref, wu.at[core], w_loc.at[0])
    down_rows = pl.ds(pl.multiple_of(core * 128, 128), 128)
    down_other = pl.ds(pl.multiple_of(other * 128, 128), 128)
    send(up_ref, wu.at[core], w_send.at[0], w_recv.at[0], partner)
    for copy in small[3:]:
        copy.wait()
    vnf[...] = vn_s[...].astype(F32)
    for n in range(R // STEP):
        requests = range(n * STEP, (n + 1) * STEP)
        values_in[n].wait()
        mixed = [
            jnp.dot(weights[r], v_s[r], preferred_element_type=F32) + own_weights[r] * vnf[r : r + 1, :]
            for r in requests
        ]
        for r, part in zip(requests, mixed):
            att[r : r + 1, :] = jnp.sum(jnp.where(mine_head, part, 0.0), axis=0, keepdims=True)
    values = (resid_s[...].astype(F32) + att[...]).astype(BF).astype(F32)

    def exchange(cb, kb):
        ca, ka = cols - cb, cols - kb
        xa = xbuf.at[:, :, :, 0:ca]
        ya, yr, yl, ra = [ref.at[:, :, 0:ka] for ref in (ya_s, yr_s, yl_s, ra_s)]
        yf, rlr = [ref.at[:, :, :, 0:ka] for ref in (yf_s, rlr_s)]
        ps, qs, rz = [ref.at[:, :, 0:ka] for ref in (ps_s, qs_s, rz_s)]
        tz = tz_s.at[:, 0:ka]
        if cb:
            xb = xb_s.at[:, :, :, 0:cb]
        if kb:
            pb, zs, tb, rxy = pb_s.at[:, :, :, 0:kb], zs_s.at[:, :, :, 0:kb], tb_s.at[:, :, 0:kb], rxy_s.at[:, :, 0:kb]
            zr = zr_s.at[:, :, :, :, 0:kb]

        def slot(i, j):
            return xa.at[(p2 + i) % 4, (p1 + j) % 4]

        def lies(k):
            return pl.ds(DIST.index(k) * R, R)

        gain = jnp.concatenate([gain_s[pl.ds(group(0, 0) * 6 + n, 1), :] for n in range(cols // 128)], axis=1)
        own_mean = jnp.mean(values, axis=1, keepdims=True)
        off = values - own_mean
        scaled = (off * gain).astype(BF)
        mine = slot(0, 0)
        mine[0:R, :] = scaled[:, :ca]
        if cb:
            mine_b = xb.at[0, p2 * 4 + p1]
            mine_b[...] = scaled[:, ca:]

        def copy1(t, c):
            rows = CHUNKS[c]
            send(slot(0, 0).at[rows], slot(0, 0).at[rows], p1_send, p1_recv.at[t - 1, c], near(0, t))

        def copy2(i, j, rows, n, c, to):
            if rows.start < rows.stop:
                sem = p2_recv.at[n, c, j] if n < 2 else p2o_recv.at[j]
                send(slot(i, j).at[rows], slot(i, j).at[rows], p2_send, sem, near(to, 0))

        def spread(j, c):
            copy2(0, j, CHUNKS[c], 0, c, 1)
            copy2(0, j, CHUNKS[c], 1, c, 3)

        def own_part(c):
            for t in (1, 3, 2):
                copy1(t, c)
            spread(0, c)

        def to_z(distances):
            for k in distances:
                send(mine.at[0:R], mine.at[lies(NZ - k)], z_send, z_recv.at[0 if k in (1, 7, 6, 2) else 1], along_z(k))

        to_z((6, 2, 1, 7))
        own_part(0)
        to_z((4, 5, 3))
        for i, j in plane if cb else []:
            send(mine_b, mine_b, xy_send, xy_recv, near(i, j))

        lane = lax.broadcasted_iota(jnp.int32, (R, 128), 1)
        line = lax.broadcasted_iota(jnp.int32, (R, 128), 0)
        g_here = group(0, 0)
        eye = (lane == (g_here % 8) * 16 + line).astype(F32)
        own_sq = jnp.sum(off * off, axis=1, keepdims=True)
        here = stats.at[g_here]
        here[0:1, :] = jnp.sum(own_mean * eye, axis=0, keepdims=True)
        here[1:2, :] = jnp.sum(own_sq * eye, axis=0, keepdims=True)
        for i, j in plane:
            send(here, here, st_send, st_recv, near(i, j))
        down_here = fetch(down_ref, wd.at[down_rows], w_loc.at[1])
        send(down_ref, wd.at[down_rows], w_send.at[1], w_recv.at[1], partner)

        for g in range(16):
            row = jnp.concatenate([gain_s[g * 6 + n : g * 6 + n + 1, :] for n in range(cols // 128)], axis=1)
            high = row.astype(BF).astype(F32)
            upper = lax.broadcasted_iota(jnp.int32, (16, cols), 0) < 8
            gb[g] = jnp.where(upper, high, row - high).astype(BF)

        block0 = z * 32 + group(0, 0)
        hit0 = jnp.max((active_s[...] == block0).astype(F32), axis=1, keepdims=True)
        hit1 = jnp.max((active_s[...] == block0 + 16).astype(F32), axis=1, keepdims=True)
        spans = active_s.shape[0]
        hits = jnp.concatenate([jnp.broadcast_to(hit0, (spans, 128)), jnp.broadcast_to(hit1, (spans, 128))], axis=1)
        row_at = lax.broadcasted_iota(jnp.int32, (ROWS, spans), 0)
        span_at = lax.broadcasted_iota(jnp.int32, (ROWS, spans), 1)
        lie = row_at // R
        away = jnp.where(lie % 2 == 1, (lie + 1) // 2, (NZ - lie // 2) % NZ)
        span_of = (((z + away) % NZ) * 2 + core) * 4 + (row_at % R) // 4
        row_mask = jnp.dot((span_of == span_at).astype(BF), hits.astype(BF), preferred_element_type=F32)
        def by_right(j, c):
            return (slice(0, 16 - 16 * (j % 2)), slice(16, 48), slice(80, 96 + 16 * (j % 2)))[c]

        def by_left(j, c):
            return (slice(16 - 16 * (j % 2), 16), slice(48, 80), slice(96 + 16 * (j % 2), 128))[c]

        def relay1(c):
            for j in (3, 1, 2):
                arrived(slot(0, j).at[CHUNKS[c]], p1_recv.at[3 - j, c])
                spread(j, c)

        def relay2(j, c):
            arrived(slot(3, j).at[CHUNKS[c]], p2_recv.at[0, c, j])
            copy2(3, j, by_right(j, c), 2, c, 1)
            arrived(slot(1, j).at[CHUNKS[c]], p2_recv.at[1, c, j])
            copy2(1, j, by_left(j, c), 3, c, 3)

        def opposite2(j):
            arrived(slot(2, j), p2o_recv.at[j])

        def up(i, j):
            g = group(i, j)
            rows = pl.ds(pl.multiple_of(g * cols, 128), ca)
            both = jnp.concatenate([wu[0, rows, :], wu[1, rows, :]], axis=1)
            if i == 2:
                return jnp.dot(slot(i, j)[...], both, preferred_element_type=F32)
            lines = jnp.concatenate([slot(i, j)[...], gb[g, :, :ca]], axis=0)
            part = jnp.dot(lines, both, preferred_element_type=F32)
            us[g] = part[ROWS:]
            return part[:ROWS]

        def gain_part(i, j):
            g = group(i, j)
            rows = pl.ds(pl.multiple_of(g * cols, 128), ca)
            both = jnp.concatenate([wu[0, rows, :], wu[1, rows, :]], axis=1)
            us[g] = jnp.dot(gb[g, :, :ca], both, preferred_element_type=F32)

        pieces = [slice(0, 8), slice(8, 16)]

        def ring_on(way, step, piece):
            at, to = ((NZ - step) % NZ, NZ - step - 1) if way == 0 else (step, step + 1)
            send(
                xb.at[at, pieces[piece]], xb.at[to, pieces[piece]],
                ring_send, ring_recv.at[way, step, piece], along_z(1 if way == 0 else NZ - 1),
            )

        def ring_in(way, step, piece):
            at = NZ - step if way == 0 else step
            arrived(xb.at[at, pieces[piece]], ring_recv.at[way, step - 1, piece])

        def ring_start():
            if not cb:
                return
            arrived(xb.at[0, 0:15], xy_recv)
            for piece in range(2):
                for way in range(2):
                    ring_on(way, 0, piece)

        def ring_relay(step, piece):
            if not cb:
                return
            for way in range(2):
                ring_in(way, step, piece)
                if step < 3 or piece == way:
                    ring_on(way, step, piece)

        def ring_end():
            ring_in(0, 4, 0)
            ring_in(1, 4, 1)

        def up_b(q2, q1):
            g = (q1 * other + q2 * core) * 4 + q2 * other + q1 * core
            rows = pl.ds(pl.multiple_of(g * cols + ca, 128), cb)
            both = jnp.concatenate([wu[0, rows, :], wu[1, rows, :]], axis=1)
            lines = jnp.concatenate([xb[k, q2 * 4 + q1] for k in DIST] + [gb[g, :, ca:]], axis=0)
            part = jnp.dot(lines, both, preferred_element_type=F32)
            us[g] = us[g] + part[ROWS:]
            return part[:ROWS]

        relay1(0)
        arrived(mine.at[CHUNKS[1]], z_recv.at[0])
        own_part(1)
        ring_start()
        arrived(mine.at[CHUNKS[2]], z_recv.at[1])
        own_part(2)
        relay2(0, 0)
        relay1(1)
        ring_relay(1, 0)
        arrived(stats.at[0:15], st_recv)
        for half in range(2):
            zst[0, 2 * half : 2 * half + 2, :] = jnp.sum(stats[8 * half : 8 * half + 8], axis=0)
        for k in range(1, NZ):
            send(zst.at[0], zst.at[NZ - k], sz_send, sz_recv, along_z(k))
        ring_relay(1, 1)
        relay2(3, 0)
        relay2(1, 0)
        relay2(2, 0)
        relay1(2)
        relay2(0, 1)
        ring_relay(2, 0)
        relay2(3, 1)
        relay2(1, 1)
        ring_relay(2, 1)
        relay2(2, 1)
        relay2(0, 2)
        ring_relay(3, 0)
        relay2(3, 2)
        ring_relay(3, 1)
        relay2(1, 2)
        relay2(2, 2)
        up_here.wait()
        arrived(wu.at[other], w_recv.at[0])
        before = up(0, 0) + up(0, 3)
        before += up(0, 1) + up(0, 2)
        before += up(3, 0) + up(1, 0)
        before += up(3, 3) + up(1, 3)
        before += up(3, 1) + up(1, 1)
        before += up(3, 2) + up(1, 2)

        arrived(zst.at[1:NZ], sz_recv)
        own_lane = lane % 16 == line
        mean_at, square_at = [
            [jnp.concatenate([jnp.where(own_lane, zst[k, 2 * half + n : 2 * half + n + 1, :], 0.0) for k in DIST], axis=0) for half in range(2)]
            for n in range(2)
        ]
        mean_row = jnp.sum(mean_at[0] + mean_at[1], axis=1, keepdims=True) * (1.0 / 16)
        lanes = lax.broadcasted_iota(jnp.int32, (ROWS, 128), 1) % 16 == lax.broadcasted_iota(jnp.int32, (ROWS, 128), 0) % 16
        gaps = [jnp.where(lanes, part - mean_row, 0.0) for part in mean_at]
        var_row = jnp.sum(
            square_at[0] + square_at[1] + cols * (gaps[0] * gaps[0] + gaps[1] * gaps[1]), axis=1, keepdims=True
        ) * (1.0 / width)
        rstd_row = lax.rsqrt(var_row + 1e-05)

        for j in range(4):
            gain_part(2, j)
        if cb:
            ring_end()
        for q in range(16) if cb else []:
            before += up_b(q // 4, q % 4)
        for half in range(2):
            gains = []
            for g in range(8 * half, 8 * half + 8):
                both = us[g, :8, :] + us[g, 8:, :]
                gains += [both, both]
            before += jnp.dot(
                gaps[half], jnp.concatenate(gains, axis=0), preferred_element_type=F32, precision=lax.Precision.HIGHEST
            )
        for j in (0, 3, 1, 2):
            opposite2(j)
            before += up(2, j)
        hidden = (jnp.maximum(before * rstd_row, 0.0) * row_mask).astype(BF)

        down_here.wait()
        arrived(wd.at[down_other], w_recv.at[1])
        back = (2, 3, 1, 0)

        def down(i, j):
            columns = pl.ds(pl.multiple_of(group(i, j) * cols, 128), ka)
            return jnp.dot(hidden, wd[:, columns], preferred_element_type=F32)

        def pass_on(src, dst, j, rows, c, to, s_sem, r_sem):
            if rows.start < rows.stop:
                send(src.at[j, rows], dst.at[j, rows], s_sem, r_sem.at[c, j], near(to, 0))

        def with_arrived(base, j, rows, out):
            if rows.start < rows.stop:
                out[j, rows, :] = (yf[base, j, rows, :] + ra[j, rows, :].astype(F32)).astype(BF)

        def alone(base, j, rows, out):
            if rows.start < rows.stop:
                out[j, rows, :] = yf[base, j, rows, :].astype(BF)

        def start_back(c, slots):
            for j in slots:
                pass_on(ya, ra, j, by_right(j, c), c, 1, a_send, a_recv)
                pass_on(ya, ra, j, by_left(j, c), c, 3, a_send, a_recv)

        def beside_back(j, c):
            alone(0, j, by_left(j, c), yr)
            alone(1, j, by_right(j, c), yl)
            arrived(ra.at[j, CHUNKS[c]], a_recv.at[c, j])
            with_arrived(0, j, by_right(j, c), yr)
            pass_on(yr, rlr.at[0], j, CHUNKS[c], c, 1, b_send.at[0], b_recv)
            with_arrived(1, j, by_left(j, c), yl)
            pass_on(yl, rlr.at[1], j, CHUNKS[c], c, 3, b_send.at[1], b_recv)

        def ring_back(way, k, piece):
            if not kb:
                return
            away = k if way == 0 else NZ - k
            part = pb[away, pieces[piece]]
            if k < 3 or (k == 3 and piece == way):
                arrived(zr.at[way, k, pieces[piece]], back_recv.at[way, k, piece])
                part += zr[way, k, pieces[piece]].astype(F32)
            zs[way * 4 + k - 1, pieces[piece]] = part.astype(BF)
            send(
                zs.at[way * 4 + k - 1, pieces[piece]], zr.at[way, k - 1, pieces[piece]],
                back_send, back_recv.at[way, k - 1, piece], along_z(1 if way == 0 else NZ - 1),
            )

        for j in back:
            ya[j] = down(2, j).astype(BF)
            start_back(2, (j,))
        start_back(0, back)
        start_back(1, back)
        for q2, q1 in [(q // 4, q % 4) for q in range(16)] if kb else []:
            g = (q1 * other + q2 * core) * 4 + q2 * other + q1 * core
            columns = pl.ds(pl.multiple_of(g * cols + ka, 128), kb)
            part = jnp.dot(hidden, wd[:, columns], preferred_element_type=F32)
            for n, k in enumerate(DIST):
                pb[k, q2 * 4 + q1] = part[n * R : (n + 1) * R]
        ring_back(0, 4, 0)
        ring_back(1, 4, 1)
        ring_back(0, 3, 1)
        ring_back(1, 3, 0)
        for j in back:
            yf[0, j] = down(1, j)
            yf[1, j] = down(3, j)
            beside_back(j, 2)
        ring_back(0, 3, 0)
        ring_back(1, 3, 1)
        for j in back:
            beside_back(j, 1)
        ring_back(0, 2, 1)
        ring_back(1, 2, 0)
        for j in back:
            beside_back(j, 0)
        ring_back(0, 2, 0)
        ring_back(1, 2, 1)
        for j in back:
            yf[2, j] = down(0, j)

        def settled(j, c):
            rows = CHUNKS[c]
            arrived(rlr.at[:, j, rows], b_recv.at[c, j])
            return yf[2, j, rows, :] + rlr[0, j, rows, :].astype(F32) + rlr[1, j, rows, :].astype(F32)

        def settle(c):
            rows = CHUNKS[c]
            for j in (2, 3, 1):
                ps[j - 1, rows, :] = settled(j, c).astype(BF)
                send(ps.at[j - 1, rows], qs.at[j - 1, rows], c_send, c_recv.at[c], near(0, j))

        def settle_own(c):
            rows = CHUNKS[c]
            part = settled(0, c)
            arrived(qs.at[:, rows], c_recv.at[c])
            for j in (3, 1, 2):
                part += qs[j - 1, rows, :].astype(F32)
            return part

        def to_owners(c, distances):
            rows = CHUNKS[c]
            tz[rows, :] = settle_own(c).astype(BF)
            for k in distances:
                send(tz.at[lies(k)], rz.at[k - 1], zz_send, zz_recv, along_z(k))

        settle(2)
        ring_back(0, 1, 1)
        ring_back(1, 1, 0)
        settle(1)
        to_owners(2, (4, 3, 5))
        ring_back(0, 1, 0)
        ring_back(1, 1, 1)
        settle(0)
        to_owners(1, (2, 6, 1, 7))
        if kb:
            for piece in range(2):
                for way in range(2):
                    arrived(zr.at[way, 0, pieces[piece]], back_recv.at[way, 0, piece])
            whole = pb[0] + zr[0, 0].astype(F32) + zr[1, 0].astype(F32)
            pb[0] = whole
            tb[...] = whole.astype(BF)
            for n, (i, j) in enumerate(plane):
                send(tb.at[(p2 + i) % 4 * 4 + (p1 + j) % 4], rxy.at[n], xyb_send, xyb_recv, near(i, j))
        total = settle_own(0) + values[:, :ka]
        if kb:
            total_b = pb[0, p2 * 4 + p1] + values[:, ka:]
        arrived(rz, zz_recv)
        for k in range(1, NZ):
            total += rz[k - 1].astype(F32)
        out_ref[:, :ka] = total.astype(BF)
        if kb:
            arrived(rxy, xyb_recv)
            for n in range(len(plane)):
                total_b += rxy[n].astype(F32)
            out_ref[:, ka:] = total_b.astype(BF)
        for src, sem in (
            (up_ref, w_send.at[0]), (down_ref, w_send.at[1]), (stats.at[0:15], st_send), (zst.at[1:NZ], sz_send),
            (mine.at[0 : ROWS - R], z_send), (xa.at[0, 0:3], p1_send), (xa.at[0:3], p2_send), (ya, a_send), (yr, b_send.at[0]), (yl, b_send.at[1]),
            (ps, c_send), (rz, zz_send),
        ):
            sent(src, sem)
        for src, sem in ((xb.at[0, 0:15], xy_send), (xb.at[0:7], ring_send)) if cb else ():
            sent(src, sem)
        for src, sem in ((zs.at[0:7], back_send), (rxy, xyb_send)) if kb else ():
            sent(src, sem)

    for n in range(2):
        pl.when(core == n)(functools.partial(exchange, *CBS[n]))


def layer(resid, query, key_new, value_new, key_cache, value_cache, lengths, norm_gain, active, up, down):
    cols = resid.shape[1]
    width = 16 * cols
    hbm = pl.BlockSpec(memory_space=pl.ANY)
    dma = pltpu.SemaphoreType.DMA
    row = pltpu.VMEM((R, cols), BF)
    row32 = pltpu.VMEM((R, cols), F32)
    cache = pltpu.VMEM((R, 128, cols), BF)
    full = pltpu.VMEM((ROWS, cols), BF)
    four = pltpu.VMEM((4, ROWS, cols), BF)
    ring = (16, R, CB)
    one = dma(())
    return pl.pallas_call(
        layer_kernel,
        out_shape=jax.ShapeDtypeStruct((R, cols), BF),
        in_specs=[hbm] * 11,
        out_specs=pl.BlockSpec(memory_space=pltpu.VMEM),
        scratch_shapes=[
            row, row, row, row, cache, cache,
            pltpu.SMEM((R,), jnp.int32),
            pltpu.VMEM((norm_gain.shape[0] // 128, 128), F32),
            pltpu.VMEM(active.shape, jnp.int32),
            row32, row32, row32, row32,
            pltpu.VMEM((4, 4, ROWS, cols), BF),
            pltpu.VMEM((2, width, 128), BF),
            pltpu.VMEM((256, width), BF),
            pltpu.VMEM((16, 2, 128), F32),
            pltpu.VMEM((16, 16, cols), BF),
            pltpu.VMEM((16, 16, 256), F32),
            pltpu.VMEM((NZ, 4, 128), F32),
            pltpu.VMEM((3, 4, ROWS, cols), F32),
            four, four, four, four,
            pltpu.VMEM((2, 4, ROWS, cols), BF),
            pltpu.VMEM((3, ROWS, cols), BF),
            pltpu.VMEM((3, ROWS, cols), BF),
            full,
            pltpu.VMEM((NZ - 1, R, cols), BF),
            pltpu.VMEM((NZ,) + ring, BF),
            pltpu.VMEM((NZ,) + ring, F32),
            pltpu.VMEM((8,) + ring, BF),
            pltpu.VMEM((2, 4) + ring, BF),
            pltpu.VMEM(ring, BF),
            pltpu.VMEM((15, R, CB), BF),
            dma((7,)), dma((R // STEP,)), dma((R // STEP,)), dma((2,)), dma((2,)), dma((2,)),
            one, one, one, one, one, dma((2,)),
            one, dma((3, 3)), one, dma((2, 3, 4)), dma((4,)),
            one, dma((3, 4)), dma((2,)), dma((3, 4)), one, dma((3,)), one, one,
            one, one, one, dma((2, 4, 2)), one, dma((2, 4, 2)), one, one,
        ],
        compiler_params=pltpu.CompilerParams(
            collective_id=0, has_side_effects=True, vmem_limit_bytes=60 * 1024 * 1024
        ),
        name="layer",
    )(resid, query, key_new, value_new, key_cache, value_cache, lengths, norm_gain.reshape(-1, 128), active, up, down)


def shards(
    resid, query, key_new, value_new, key_cache, value_cache, lengths, norm_gain, active, up_weight, down_weight
):
    return layer(
        resid, query, key_new, value_new, key_cache, value_cache, lengths, norm_gain, active, up_weight, down_weight
    )


def solution(mesh):
    placed = (
        P("attn", ("ffn", "grp")),
        P("attn", ("ffn", "grp")),
        P("attn", ("ffn", "grp")),
        P("attn", ("ffn", "grp")),
        P("attn", None, ("ffn", "grp")),
        P("attn", None, ("ffn", "grp")),
        P("attn"),
        P(),
        P(),
        P(None, ("attn", "ffn", "grp")),
        P(("attn", "ffn", "grp"), None),
    )
    return jax.shard_map(
        shards, mesh=mesh, in_specs=placed, out_specs=P("attn", ("ffn", "grp")), check_vma=False
    )
```

time: 70.2 us -> 61.2 us (0.87)
  Pallas kernels: 68.7 us -> 59.8 us
    pallas_call x1, Pallas kernels: 68.7 us -> 59.8 us  [layer(): pl.pallas_call(layer_kernel, out_shape=jax.ShapeDtypeStruct((R, cols), BF...]
where the time goes in v4:
time: 61.2 us; the launch traced here: 61.1 us
  Pallas kernels  59.8 us (98%)
  local copies, waits for them, and re-layouts  1.35 us (2%)
    pallas_call x1, Pallas kernels, layer(): pl.pallas_call(layer_kernel, out_shape=jax.ShapeDtypeStruct((R, cols), BF...  59.8 us
    unnamed x1, local copies, waits for them, and re-layouts  1.35 us

profile of v4, /device:TPU:2, one launch (start us, length us, event | category | flops | bytes accessed | tf_op | source)
XLA Modules:
  0.0 61.1 jit_solution(1981559413327067565)
XLA Ops:
  0.0 59.8 %layer.1 = bf16[16,768]{1,0:T(8,128)(2,1)} custom-call(bf16[16,768]{1,0:T(8,128)(2,1)} %resid_ref.1, bf16[16,768]{1,0:T(8,128)(2,1)} %q_ref.1, bf16[16,768]{1,0:T(8,128)(2,1)} %kn_ref.1, bf16[16,768]{1,0:T(8,128)(2,1)} %vn_ref.1, bf16[16,128,768]{2,1,0:T(8,128)(2,1)} %k_ref.1, bf16[16,128,768]{2,1,0:T(8,128)(2,1)} %v_ref.1, s32[16]{0:T(128)} %len_ref.1, ...), custom_call_target="tpu_custom_call" | custom-call | tf_op jit(solution)/shard_map/layer/pallas_call | solution.py:543
  59.8 1.3 %copy.13 = bf16[16,768]{1,0:T(8,128)(2,1)} copy(bf16[16,768]{1,0:T(8,128)(2,1)} %layer.1) | data formatting | bytes 49152

commit v5 on v4

--- a/solution.py
+++ b/solution.py
@@ -17,7 +17,7 @@
 ROWS = R * NZ
 DIST = (0, 1, 7, 2, 6, 3, 5, 4)
 STEP = 4
-CBS = ((0, 0), (256, 384))
+CBS = ((0, 128), (256, 256))
 CB = max(CBS[0] + CBS[1])
 CHUNKS = (slice(0, 16), slice(16, 80), slice(80, 128))
 
@@ -121,10 +121,8 @@
         weights += [(e / d).astype(BF) for e, d in zip(expo, denom)]
         own_weights += [(o / d).astype(BF).astype(F32) for o, d in zip(own, denom)]
     pl.semaphore_wait(barrier, len(plane) + NZ)
-    up_here = fetch(up_ref, wu.at[core], w_loc.at[0])
     down_rows = pl.ds(pl.multiple_of(core * 128, 128), 128)
     down_other = pl.ds(pl.multiple_of(other * 128, 128), 128)
-    send(up_ref, wu.at[core], w_send.at[0], w_recv.at[0], partner)
     for copy in small[3:]:
         copy.wait()
     vnf[...] = vn_s[...].astype(F32)
@@ -137,6 +135,8 @@
         ]
         for r, part in zip(requests, mixed):
             att[r : r + 1, :] = jnp.sum(jnp.where(mine_head, part, 0.0), axis=0, keepdims=True)
+    up_here = fetch(up_ref, wu.at[core], w_loc.at[0])
+    send(up_ref, wu.at[core], w_send.at[0], w_recv.at[0], partner)
     values = (resid_s[...].astype(F32) + att[...]).astype(BF).astype(F32)
 
     def exchange(cb, kb):

time: 61.2 us -> 60.7 us (level)
  Pallas kernels: 59.8 us -> 59.1 us
    pallas_call x1, Pallas kernels: 59.8 us -> 59.1 us  [layer(): pl.pallas_call(layer_kernel, out_shape=jax.ShapeDtypeStruct((R, cols), BF...]
where the time goes in v5:
time: 60.7 us; the launch traced here: 60.4 us
  Pallas kernels  59.1 us (97%)
  local copies, waits for them, and re-layouts  1.35 us (2%)
    pallas_call x1, Pallas kernels, layer(): pl.pallas_call(layer_kernel, out_shape=jax.ShapeDtypeStruct((R, cols), BF...  59.1 us
    unnamed x1, local copies, waits for them, and re-layouts  1.35 us

profile of v5, /device:TPU:2, one launch (start us, length us, event | category | flops | bytes accessed | tf_op | source)
XLA Modules:
  0.0 60.4 jit_solution(16047856263156157373)
XLA Ops:
  0.0 59.1 %layer.1 = bf16[16,768]{1,0:T(8,128)(2,1)} custom-call(bf16[16,768]{1,0:T(8,128)(2,1)} %resid_ref.1, bf16[16,768]{1,0:T(8,128)(2,1)} %q_ref.1, bf16[16,768]{1,0:T(8,128)(2,1)} %kn_ref.1, bf16[16,768]{1,0:T(8,128)(2,1)} %vn_ref.1, bf16[16,128,768]{2,1,0:T(8,128)(2,1)} %k_ref.1, bf16[16,128,768]{2,1,0:T(8,128)(2,1)} %v_ref.1, s32[16]{0:T(128)} %len_ref.1, ...), custom_call_target="tpu_custom_call" | custom-call | tf_op jit(solution)/shard_map/layer/pallas_call | solution.py:543
  59.1 1.3 %copy.13 = bf16[16,768]{1,0:T(8,128)(2,1)} copy(bf16[16,768]{1,0:T(8,128)(2,1)} %layer.1) | data formatting | bytes 49152
